TPU v7x, 256 devices: a whole 4x4x8 slice. The times are simulated.
256 devices in a mesh: section: 4 (over z_hi), vit: 16 (over y, x), dp: 4 (over z_lo, core).
Axes of the slice: x: 4, y: 4, z: 8 (z_hi: 4, z_lo: 2; z = z_hi * 2 + z_lo), core: 2. Of those that a mesh axis runs over, the one named last changes fastest.
Arguments:
- grad_llm: bfloat16 [4, 8192, 4096], P('section', ('dp', 'vit')), parts along dimension 1, may hold values from -6 to 6
- vis_slot: int32 [64, 128], P('dp'), parts along dimension 0, may hold values from 0 to 2047, as said below
- image_rows: int32 [16, 16], P('dp'), parts along dimension 0, may hold values from 8 to 32, as said below
- section_layer: int32 [4], replicated, may hold values from 0 to 3, each once
- vit_in: bfloat16 [32768, 1152], P(('dp', 'section', 'vit')), parts along dimension 0, may hold values from -6 to 6
- vit_out: bfloat16 [32768, 1152], P(('dp', 'section', 'vit')), parts along dimension 0, may hold values from -6 to 6
- ln_gain: float32 [1152], replicated, may hold values from 0.5 to 1.5
- ln_bias: float32 [1152], replicated, may hold values from -3 to 3
- qkv_weight: bfloat16 [1152, 3456], P('section'), may hold values from -0.1875 to 0.1875
- proj_weight: bfloat16 [1152, 1152], P('section'), may hold values from -0.1875 to 0.1875
- merge_gain: float32 [1152], replicated, may hold values from 0.5 to 1.5
- merge_bias: float32 [1152], replicated, may hold values from -3 to 3
- fc1_weight: bfloat16 [4608, 4608], P(None, 'vit'), may hold values from -0.09375 to 0.09375
- fc1_bias: float32 [4608], P('vit'), may hold values from -3 to 3
- fc2_weight: bfloat16 [4608, 4096], P('vit'), may hold values from -0.09375 to 0.09375
Outputs:
- vit_grad: bfloat16 [32768, 1152], P(('dp', 'section', 'vit')), parts along dimension 0
There are 4 independent parts, one for each index of `dp`. A program takes and returns all parts, laid end to end along the dimension named above; an argument that names none is the same for every part. Nothing has to cross between parts.
Inputs may be any that keep to these rules, and one draw needn't show every extreme that they name: `vis_slot`: every slot number appears once. On every language-model device v, the rows d * 2 to d * 2 + 1 name 2 consecutive slots that start at a multiple of 2 inside d * 32 to d * 32 + 31, the slots of vision device d (devices numbered with the group first). `image_rows`: in every group one image has exactly 32 merged tokens. `section_layer`: A permutation; the section with value 3 holds no DeepStack layer.
All inputs are finite; a program needn't handle non-finite values.
Results may differ from a plain program's by a relative error of at most 0.02.
Values may be sent and summed in bfloat16 or wider, within the bound.
A program may use at most 128 MiB of HBM per device.

v0:
```python
import jax
import jax.numpy as jnp
from jax import lax
from jax.sharding import PartitionSpec as P

HEADS = 16
LEVELS = 3


norm_eps = 1e-06


def normalize(values):
    row_mean = jnp.mean(values, axis=-1, keepdims=True)
    centered = values - row_mean
    variance = jnp.mean(centered * centered, axis=-1, keepdims=True)
    inverse = lax.rsqrt(variance + norm_eps)
    return (centered * inverse, inverse)


def normalize_back(upstream, normed_rows, inverse, gain):
    scaled = upstream * gain
    mean_scaled = jnp.mean(scaled, axis=-1, keepdims=True)
    mean_cross = jnp.mean(scaled * normed_rows, axis=-1, keepdims=True)
    return (scaled - mean_scaled - normed_rows * mean_cross) * inverse


def gelu_slope(pre_act):
    cumulative = 0.5 * (1.0 + lax.erf(pre_act * 0.7071067811865476))
    density = jnp.exp(-0.5 * pre_act * pre_act) * 0.3989422804014327
    return cumulative + pre_act * density


def local(
    grad_llm,
    vis_slot,
    image_rows,
    section_layer,
    vit_in,
    vit_out,
    ln_gain,
    ln_bias,
    qkv_weight,
    proj_weight,
    merge_gain,
    merge_bias,
    fc1_weight,
    fc1_bias,
    fc2_weight,
):
    sections = lax.axis_size("section")
    shards = lax.axis_size("vit")
    section_index = lax.axis_index("section")
    shard_index = lax.axis_index("vit")
    devices = sections * shards
    patches = vit_in.shape[0]
    slots_here = patches // 4
    run_rows = grad_llm.shape[1] // devices
    llm_width = grad_llm.shape[2]
    vit_width = vit_in.shape[1]
    head_dim = vit_width // HEADS
    device_index = section_index * shards + shard_index
    qkv_full, proj_full = (
        lax.all_gather(qkv_weight, "section", axis=0, tiled=True),
        lax.all_gather(proj_weight, "section", axis=0, tiled=True),
    )
    in_rows, in_inverse = normalize(vit_in.astype(jnp.float32))
    normed = (in_rows * ln_gain + ln_bias).astype(jnp.bfloat16)
    projected = lax.dot_general(
        qkv_full, normed, (((0,), (1,)), ((), ())), preferred_element_type=jnp.float32
    )
    projected = projected.astype(jnp.bfloat16).reshape(3, HEADS, head_dim, patches)
    section_weight = jnp.where(
        section_layer < LEVELS, (section_layer + 1).astype(jnp.float32) / LEVELS, 0.0
    )
    outgoing = grad_llm[0].reshape(devices, run_rows, llm_width)
    image_ends = jnp.cumsum(image_rows[section_index])
    out_rows, out_inverse = normalize(vit_out.astype(jnp.float32))
    merge_in = (
        (out_rows * merge_gain + merge_bias).astype(jnp.bfloat16).reshape(slots_here, 4 * vit_width)
    )
    arrived = lax.all_to_all(outgoing, ("section", "vit"), split_axis=0, concat_axis=0, tiled=True)
    arrived_f = arrived.reshape(sections, shards, run_rows, llm_width).astype(jnp.float32)
    incoming = jnp.sum(arrived_f * section_weight[:, None, None, None], axis=0)
    columns = lax.dynamic_slice_in_dim(vis_slot, device_index * run_rows, run_rows, 1)
    local_slot = (columns - device_index * slots_here).reshape(-1)
    placed = (
        jnp.zeros((slots_here, llm_width), jnp.float32)
        .at[local_slot]
        .set(incoming.reshape(-1, llm_width))
    )
    slot_position = shard_index * slots_here + jnp.arange(slots_here, dtype=jnp.int32)
    merged_grad = jnp.where((slot_position < image_ends[-1])[:, None], placed, 0.0).astype(
        jnp.bfloat16
    )
    rows_in, rows_grad = (
        lax.all_gather(merge_in, "vit", axis=0, tiled=True),
        lax.all_gather(merged_grad, "vit", axis=0, tiled=True),
    )
    pre_act = jnp.dot(rows_in, fc1_weight, preferred_element_type=jnp.float32) + fc1_bias
    hidden_grad = lax.dot_general(
        rows_grad, fc2_weight, (((1,), (1,)), ((), ())), preferred_element_type=jnp.float32
    )
    pre_grad = (hidden_grad * gelu_slope(pre_act)).astype(jnp.bfloat16)
    merge_grad = lax.psum_scatter(
        lax.dot_general(
            pre_grad, fc1_weight, (((1,), (1,)), ((), ())), preferred_element_type=jnp.float32
        ).astype(jnp.bfloat16),
        "vit",
        scatter_dimension=0,
        tiled=True,
    ).astype(jnp.float32)
    out_grad = normalize_back(
        merge_grad.reshape(patches, vit_width), out_rows, out_inverse, merge_gain
    ).astype(jnp.bfloat16)
    grad_cols = lax.dot_general(
        proj_full, out_grad, (((1,), (1,)), ((), ())), preferred_element_type=jnp.float32
    )
    grad_cols = grad_cols.astype(jnp.bfloat16).reshape(1, HEADS, head_dim, patches)
    head_inputs, head_grad = (
        lax.all_to_all(projected, "vit", split_axis=1, concat_axis=3, tiled=True),
        lax.all_to_all(grad_cols, "vit", split_axis=1, concat_axis=3, tiled=True),
    )
    length = shards * patches
    block_size = min(512, length)
    block_count = length // block_size
    slot_of = jnp.arange(length, dtype=jnp.int32) // 4
    patch_image = jnp.sum((slot_of[:, None] >= image_ends[None, :]).astype(jnp.int32), axis=1)
    patch_live = slot_of < image_ends[-1]
    score_scale = head_dim ** (-0.5)
    contract_first = (((0,), (0,)), ((), ()))

    def head_backward(query_cols, key_cols, value_cols, grad_head):

        def step(carry, block_index):
            key_acc, value_acc = carry
            first_row = block_index * block_size
            query_block = lax.dynamic_slice_in_dim(query_cols, first_row, block_size, 1)
            grad_block = lax.dynamic_slice_in_dim(grad_head, first_row, block_size, 1)
            image_block = lax.dynamic_slice_in_dim(patch_image, first_row, block_size, 0)
            live_block = lax.dynamic_slice_in_dim(patch_live, first_row, block_size, 0)
            scores = (
                lax.dot_general(
                    query_block, key_cols, contract_first, preferred_element_type=jnp.float32
                )
                * score_scale
            )
            allowed = (
                (image_block[:, None] == patch_image[None, :])
                & live_block[:, None]
                & patch_live[None, :]
            )
            exponent = jnp.where(allowed, jnp.exp(jnp.where(allowed, scores, 0.0)), 0.0)
            denominator = (
                jnp.sum(exponent, axis=1, keepdims=True)
                + 1.0
                - live_block.astype(jnp.float32)[:, None]
            )
            softmax_weights = (exponent / denominator).astype(jnp.bfloat16)
            prob_grad = lax.dot_general(
                grad_block, value_cols, contract_first, preferred_element_type=jnp.float32
            )
            weighted = softmax_weights.astype(jnp.float32)
            row_dot = jnp.sum(weighted * prob_grad, axis=1, keepdims=True)
            score_grad = (weighted * (prob_grad - row_dot) * score_scale).astype(jnp.bfloat16)
            query_grad = lax.dot_general(
                key_cols, score_grad, (((1,), (1,)), ((), ())), preferred_element_type=jnp.float32
            )
            key_acc = key_acc + lax.dot_general(
                query_block,
                score_grad,
                (((1,), (0,)), ((), ())),
                preferred_element_type=jnp.float32,
            )
            value_acc = value_acc + lax.dot_general(
                grad_block,
                softmax_weights,
                (((1,), (0,)), ((), ())),
                preferred_element_type=jnp.float32,
            )
            return ((key_acc, value_acc), query_grad.astype(jnp.bfloat16))

        empty = jnp.zeros((head_dim, length), jnp.float32)
        (key_total, value_total), query_blocks = lax.scan(
            step, (empty, empty), jnp.arange(block_count, dtype=jnp.int32)
        )
        query_total = query_blocks.transpose(1, 0, 2).reshape(head_dim, length)
        return (query_total, key_total.astype(jnp.bfloat16), value_total.astype(jnp.bfloat16))

    query_all, key_all, value_all = jax.vmap(head_backward)(
        head_inputs[0], head_inputs[1], head_inputs[2], head_grad[0]
    )
    head_result = jnp.stack([query_all, key_all, value_all])
    returned = lax.all_to_all(head_result, "vit", split_axis=3, concat_axis=1, tiled=True)
    projected_grad = returned.reshape(3 * vit_width, patches)
    normed_grad = lax.dot_general(
        projected_grad, qkv_full, (((0,), (1,)), ((), ())), preferred_element_type=jnp.float32
    )
    vit_grad = out_grad.astype(jnp.float32) + normalize_back(
        normed_grad, in_rows, in_inverse, ln_gain
    )
    return vit_grad.astype(jnp.bfloat16)


def solution(mesh):
    placed = (
        P("section", ("dp", "vit"), None),
        P("dp", None),
        P("dp", None),
        P(),
        P(("dp", "section", "vit"), None),
        P(("dp", "section", "vit"), None),
        P(),
        P(),
        P("section", None),
        P("section", None),
        P(),
        P(),
        P(None, "vit"),
        P("vit"),
        P("vit", None),
    )
    return jax.shard_map(
        local,
        mesh=mesh,
        in_specs=placed,
        out_specs=P(("dp", "section", "vit"), None),
        check_vma=False,
    )
```

profile of v0, /device:TPU:64, one launch (start us, length us, event | category | flops | bytes accessed | tf_op | source)
XLA Modules:
  0.0 582.3 jit_solution(12822066570429436791)
XLA Ops:
  11.7 2.5 reshape_squeeze.3
  14.2 14.1 %all-to-all-start = ((bf16[64,2,4096]{2,1,0:T(2,128)(2,1)}), bf16[64,2,4096]{2,1,0:T(2,128)(2,1)}, u32[]{:S(2)}, u32[]{:S(2)}) async-start(bf16[64,2,4096]{2,1,0:T(2,128)(2,1)} %reshape_squeeze.3), calls=%async_computation | async-start | bytes 2097152 | tf_op jit(solution)/shard_map/all_to_all | solution.py:82
  30.6 24.7 %all-to-all-done = bf16[64,2,4096]{2,1,0:T(2,128)(2,1)} async-done(((bf16[64,2,4096]{2,1,0:T(2,128)(2,1)}), bf16[64,2,4096]{2,1,0:T(2,128)(2,1)}, u32[]{:S(2)}, u32[]{:S(2)}) %all-to-all-start) | async-done | bytes 1048608 | tf_op jit(solution)/shard_map/all_to_all | solution.py:82
  55.3 2.8 fusion.25
  59.2 1.5 scatter_custom_fusion
  62.4 17.8 %all-gather.7.cloned.1.call-done = bf16[512,4608]{1,0:T(8,128)(2,1)} async-done(((bf16[32,4608]{1,0:T(8,128)(2,1)}), bf16[512,4608]{1,0:T(8,128)(2,1)}) %all-gather.7.cloned.1.call-update) | async-done | bytes 4718608 | tf_op jit(solution)/shard_map/all_gather | solution.py:97
  80.2 4.7 convolution_add_fusion
  84.9 54.0 %all-gather.5.cloned.1.call-done = bf16[512,4096]{1,0:T(8,128)(2,1)} async-done(((bf16[32,4096]{1,0:T(8,128)(2,1)}), bf16[512,4096]{1,0:T(8,128)(2,1)}) %all-gather.5.cloned.1.call-update) | async-done | bytes 4194320 | tf_op jit(solution)/shard_map/all_gather | solution.py:98
  139.0 9.2 %convolution_convert_fusion.1 = bf16[512,4608]{1,0:T(8,128)(2,1)} fusion(bf16[4608,288]{0,1:T(8,128)(2,1)S(1)} %copy-done, bf16[512,4096]{1,0:T(8,128)(2,1)} %all-gather.5.cloned.1.call-done, bf16[288,4096]{1,0:T(8,128)(2,1)} %param.31, f32[512,288]{0,1:T(8,128)} %convolution_add_fusion), kind=kOutput, calls=%fused_computation.33 | convolution fusion | flops 2570747904 | bytes 14516224 | tf_op jit(solution)/shard_map/dot_general | solution.py:106
  149.5 138.9 %all-gather.9.cloned.1.call-done = bf16[1152,3456]{1,0:T(8,128)(2,1)} async-done(((bf16[288,3456]{1,0:T(8,128)(2,1)}), bf16[1152,3456]{1,0:T(8,128)(2,1)}) %all-gather.9.cloned.1.call-update) | async-done | bytes 7962640 | tf_op jit(solution)/shard_map/all_gather | solution.py:64
  288.5 4.7 fusion.23
  295.2 6.4 %all-to-all-start.1 = ((bf16[3,16,72,128]{3,2,0,1:T(8,128)(2,1)}), bf16[3,16,72,128]{3,2,0,1:T(8,128)(2,1)S(1)}, u32[]{:S(2)}, u32[]{:S(2)}) async-start(bf16[3,16,72,128]{3,2,0,1:T(8,128)(2,1)} %copy.74), calls=%async_computation.2 | async-start | bytes 1769472 | tf_op jit(solution)/shard_map/all_to_all | solution.py:121
  301.8 78.4 %reduce-scatter.2.cloned.1.call-done = bf16[32,4608]{1,0:T(8,128)(2,1)} async-done(((bf16[512,4608]{1,0:T(8,128)(2,1)}), bf16[32,4608]{1,0:T(8,128)(2,1)}) %reduce-scatter.2.cloned.1.call-update) | async-done | bytes 294928 | tf_op jit(solution)/shard_map/reduce_scatter | solution.py:105
  381.7 60.4 %all-gather.11.cloned.1.call-done = bf16[1152,1152]{1,0:T(8,128)(2,1)} async-done(((bf16[288,1152]{1,0:T(8,128)(2,1)}), bf16[1152,1152]{1,0:T(8,128)(2,1)}) %all-gather.11.cloned.1.call-update) | async-done | bytes 2654224 | tf_op jit(solution)/shard_map/all_gather | solution.py:65
  442.1 2.7 fusion.24
  445.7 6.9 %all-to-all-start.2 = ((bf16[1,16,72,128]{3,2,0,1:T(8,128)(2,1)}), bf16[1,16,72,128]{3,2,0,1:T(8,128)(2,1)S(1)}, u32[]{:S(2)}, u32[]{:S(2)}) async-start(bf16[1,16,72,128]{3,2,0,1:T(8,128)(2,1)} %bitcast.11), calls=%async_computation.3 | async-start | bytes 589824 | tf_op jit(solution)/shard_map/all_to_all | solution.py:122
  455.3 6.5 %all-to-all-done.2 = bf16[1,16,72,128]{3,2,0,1:T(8,128)(2,1)S(1)} async-done(((bf16[1,16,72,128]{3,2,0,1:T(8,128)(2,1)}), bf16[1,16,72,128]{3,2,0,1:T(8,128)(2,1)S(1)}, u32[]{:S(2)}, u32[]{:S(2)}) %all-to-all-start.2) | async-done | bytes 294944 | tf_op jit(solution)/shard_map/all_to_all | solution.py:122
  462.7 69.6 %while.17 = (s32[]{:T(128)}, f32[1,72,2048]{2,1,0:T(8,128)S(1)}, f32[1,72,2048]{2,1,0:T(8,128)}, bf16[4,1,72,512]{3,2,1,0:T(8,128)(2,1)}, s32[4]{0:T(128)S(1)}, ...) while((s32[]{:T(128)}, f32[1,72,2048]{2,1,0:T(8,128)S(1)}, ...), condition=%wide.region_14.15_spmd.clone, body=%wide.region_11.14_spmd.clone.sunk | while | flops 773427712 | bytes 49783604 | solution.py:184
  464.7 3.5 fusion.116
  468.3 2.9 fusion.117
  471.2 1.4 copy-done.2
  473.3 2.3 fusion.119
  475.6 1.4 fusion.121
  477.0 2.9 fusion.120
  482.0 3.5 fusion.116
  485.5 2.9 fusion.117
  488.5 1.4 copy-done.2
  490.5 2.3 fusion.119
  492.8 1.4 fusion.121
  494.2 3.1 fusion.120
  499.4 3.5 fusion.116
  503.0 2.9 fusion.117
  505.9 1.4 copy-done.2
  508.0 2.3 fusion.119
  510.3 1.4 fusion.121
  511.7 3.1 fusion.120
  516.9 3.4 fusion.116
  520.4 2.9 fusion.117
  523.3 1.4 copy-done.2
  525.4 2.3 fusion.119
  527.7 1.4 fusion.121
  529.1 3.1 fusion.120
  535.8 2.9 copy.82
  538.6 3.7 reshape.278
  542.3 19.3 %all_to_all.50 = bf16[16,2,13824]{2,1,0:T(2,128)(2,1)} all-to-all(bf16[16,2,13824]{2,1,0:T(2,128)(2,1)} %reshape.278), channel_id=1, replica_groups=mesh['section'=4,'vit'=16,'dp'=4] {'vit'}, dimensions={0} | all-to-all | bytes 1769472 | tf_op jit(solution)/shard_map/all_to_all | solution.py:194
  561.6 4.4 reshape.279
  566.0 2.2 copy.86
  568.3 6.3 %fusion.83 = (f32[128]{0:T(128)S(1)}, f32[128]{0:T(128)S(1)}, f32[128,1152]{1,0:T(8,128)S(1)}) fusion(f32[128]{0:T(128)S(1)} %copy-done.22, f32[128]{0:T(128)S(1)} %copy-done.15, bf16[128,1152]{1,0:T(8,128)(2,1)S(1)} %copy-done.6, f32[1152]{0:T(1024)S(1)} %copy-done.10, bf16[3456,128]{1,0:T(8,128)(2,1)} %bitcast.134, ...), kind=kOutput, calls=%fused_computation.126 | convolution fusion | flops 1020247808 | bytes 9738752 | tf_op jit(solution)/shard_map/dot_general | solution.py:196
  (157 shorter events, 33.0 us)
Async XLA Ops:
  6.5 73.7 %copy-start = (bf16[4608,288]{0,1:T(8,128)(2,1)S(1)}, bf16[4608,288]{0,1:T(8,128)(2,1)}, u32[]{:S(2)}) copy-start(bf16[4608,288]{0,1:T(8,128)(2,1)} %param.29) | copy-start | bytes 7962628
  6.5 21.8 %copy-start.17 = (s32[16,128]{1,0:T(8,128)S(1)}, s32[16,128]{1,0:T(8,128)}, u32[]{:S(2)}) copy-start(s32[16,128]{1,0:T(8,128)} %param.18) | copy-start | bytes 24580
  6.5 24.0 %copy-start.28 = (s32[4]{0:T(128)S(1)}, s32[4]{0:T(128)}, u32[]{:S(2)}) copy-start(s32[4]{0:T(128)} %param.20) | copy-start | bytes 52
  6.5 73.7 %all-gather.7.cloned.1.call-start = ((), (), s32[]{:S(2)}) async-start(), calls=%async_computation.6 | async-start | bytes 5013504 | tf_op jit(solution)/shard_map/all_gather | solution.py:97
  7.8 1.2 copy-start.11
  9.0 0.5 copy-start.18
  14.2 66.0 %copy-start.27 = (f32[288]{0:T(512)S(1)}, f32[288]{0:T(512)}, u32[]{:S(2)}) copy-start(f32[288]{0:T(512)} %param.30) | copy-start | bytes 3460
  14.2 41.1 %all-to-all-start = ((bf16[64,2,4096]{2,1,0:T(2,128)(2,1)}), bf16[64,2,4096]{2,1,0:T(2,128)(2,1)}, u32[]{:S(2)}, u32[]{:S(2)}) async-start(bf16[64,2,4096]{2,1,0:T(2,128)(2,1)} %reshape_squeeze.3), calls=%async_computation | async-start | bytes 2097152 | tf_op jit(solution)/shard_map/all_to_all | solution.py:82
  28.3 110.7 %all-gather.5.cloned.1.call-start = ((), (), s32[]{:S(2)}) async-start(), calls=%async_computation.5 | async-start | bytes 4456448 | tf_op jit(solution)/shard_map/all_gather | solution.py:98
  61.6 226.9 %all-gather.9.cloned.1.call-start = ((), (), s32[]{:S(2)}) async-start(), calls=%async_computation.8 | async-start | bytes 9953280 | tf_op jit(solution)/shard_map/all_gather | solution.py:64
  62.3 317.9 %reduce-scatter.2.cloned.1.call-start = ((), (), s32[]{:S(2)}) async-start(), calls=%async_computation.7 | async-start | bytes 5013504 | tf_op jit(solution)/shard_map/reduce_scatter | solution.py:105
  148.2 1.0 copy-start.5
  148.2 140.3 %copy-start.10 = (f32[1152]{0:T(1024)S(1)}, f32[1152]{0:T(1024)}, u32[]{:S(2)}) copy-start(f32[1152]{0:T(1024)} %param.23) | copy-start | bytes 13828
  148.2 140.3 %copy-start.16 = (f32[1152]{0:T(1024)S(1)}, f32[1152]{0:T(1024)}, u32[]{:S(2)}) copy-start(f32[1152]{0:T(1024)} %param.24) | copy-start | bytes 13828
  148.2 293.9 %all-gather.11.cloned.1.call-start = ((), (), s32[]{:S(2)}) async-start(), calls=%async_computation.9 | async-start | bytes 3317760 | tf_op jit(solution)/shard_map/all_gather | solution.py:65
  149.3 143.9 %copy-start.14 = (f32[128]{0:T(128)}, f32[128]{0:T(128)S(1)}, u32[]{:S(2)}) copy-start(f32[128]{0:T(128)S(1)} %broadcast_multiply_fusion.2) | copy-start | bytes 1540
  149.5 143.7 %copy-start.21 = (f32[128]{0:T(128)}, f32[128]{0:T(128)S(1)}, u32[]{:S(2)}) copy-start(f32[128]{0:T(128)S(1)} %add_rsqrt_fusion) | copy-start | bytes 1540
  293.2 88.2 %copy-start.4 = (bf16[128,1152]{1,0:T(8,128)(2,1)S(1)}, bf16[128,1152]{1,0:T(8,128)(2,1)}, u32[]{:S(2)}) copy-start(bf16[128,1152]{1,0:T(8,128)(2,1)} %param.22) | copy-start | bytes 884740
  293.2 88.2 %copy-start.9 = (f32[1152]{0:T(1024)S(1)}, f32[1152]{0:T(1024)}, u32[]{:S(2)}) copy-start(f32[1152]{0:T(1024)} %param.27) | copy-start | bytes 13828
  293.2 88.2 %copy-start.12 = (f32[128]{0:T(128)S(1)}, f32[128]{0:T(128)}, u32[]{:S(2)}) copy-start(f32[128]{0:T(128)} %copy-done.11) | copy-start | bytes 1540
  293.2 88.2 %copy-start.19 = (f32[128]{0:T(128)S(1)}, f32[128]{0:T(128)}, u32[]{:S(2)}) copy-start(f32[128]{0:T(128)} %copy-done.18) | copy-start | bytes 1540
  295.2 150.4 %all-to-all-start.1 = ((bf16[3,16,72,128]{3,2,0,1:T(8,128)(2,1)}), bf16[3,16,72,128]{3,2,0,1:T(8,128)(2,1)S(1)}, u32[]{:S(2)}, u32[]{:S(2)}) async-start(bf16[3,16,72,128]{3,2,0,1:T(8,128)(2,1)} %copy.74), calls=%async_computation.2 | async-start | bytes 1769472 | tf_op jit(solution)/shard_map/all_to_all | solution.py:121
  381.4 71.1 %copy-start.7 = (f32[128,1152]{1,0:T(8,128)}, f32[128,1152]{1,0:T(8,128)S(1)}, u32[]{:S(2)}) copy-start(f32[128,1152]{1,0:T(8,128)S(1)} %reshape.258) | copy-start | bytes 1769476
  381.7 72.6 %copy-start.23 = (f32[128]{0:T(128)}, f32[128]{0:T(128)S(1)}, u32[]{:S(2)}) copy-start(f32[128]{0:T(128)S(1)} %get-tuple-element.160) | copy-start | bytes 1540
  381.7 72.6 %copy-start.25 = (f32[128]{0:T(128)}, f32[128]{0:T(128)S(1)}, u32[]{:S(2)}) copy-start(f32[128]{0:T(128)S(1)} %get-tuple-element.161) | copy-start | bytes 1540
  445.7 16.1 %all-to-all-start.2 = ((bf16[1,16,72,128]{3,2,0,1:T(8,128)(2,1)}), bf16[1,16,72,128]{3,2,0,1:T(8,128)(2,1)S(1)}, u32[]{:S(2)}, u32[]{:S(2)}) async-start(bf16[1,16,72,128]{3,2,0,1:T(8,128)(2,1)} %bitcast.11), calls=%async_computation.3 | async-start | bytes 589824 | tf_op jit(solution)/shard_map/all_to_all | solution.py:122
  471.2 1.4 copy-start.2
  473.3 3.7 copy-start.3
  488.4 1.4 copy-start.2
  490.5 3.7 copy-start.3
  505.9 1.4 copy-start.2
  508.0 3.7 copy-start.3
  523.3 1.4 copy-start.2
  525.4 3.7 copy-start.3
  542.3 25.9 %copy-start.6 = (bf16[128,1152]{1,0:T(8,128)(2,1)S(1)}, bf16[128,1152]{1,0:T(8,128)(2,1)}, u32[]{:S(2)}) copy-start(bf16[128,1152]{1,0:T(8,128)(2,1)} %param.21) | copy-start | bytes 884740
  542.3 25.9 %copy-start.15 = (f32[128]{0:T(128)S(1)}, f32[128]{0:T(128)}, u32[]{:S(2)}) copy-start(f32[128]{0:T(128)} %copy-done.14) | copy-start | bytes 1540
  542.3 25.9 %copy-start.22 = (f32[128]{0:T(128)S(1)}, f32[128]{0:T(128)}, u32[]{:S(2)}) copy-start(f32[128]{0:T(128)} %copy-done.21) | copy-start | bytes 1540
  568.2 7.6 %copy-start.1 = (bf16[4608,288]{0,1:T(8,128)(2,1)S(1)}, bf16[4608,288]{0,1:T(8,128)(2,1)}, u32[]{:S(2)}) copy-start(bf16[4608,288]{0,1:T(8,128)(2,1)} %param.29) | copy-start | bytes 7962628
  568.2 6.4 %copy-start.8 = (f32[128,1152]{1,0:T(8,128)S(1)}, f32[128,1152]{1,0:T(8,128)}, u32[]{:S(2)}) copy-start(f32[128,1152]{1,0:T(8,128)} %copy-done.7) | copy-start | bytes 1769476
  568.2 6.4 %copy-start.13 = (f32[128]{0:T(128)S(1)}, f32[128]{0:T(128)}, u32[]{:S(2)}) copy-start(f32[128]{0:T(128)} %copy-done.11) | copy-start | bytes 1540
  568.2 6.4 %copy-start.20 = (f32[128]{0:T(128)S(1)}, f32[128]{0:T(128)}, u32[]{:S(2)}) copy-start(f32[128]{0:T(128)} %copy-done.18) | copy-start | bytes 1540
  568.3 6.4 %copy-start.24 = (f32[128]{0:T(128)S(1)}, f32[128]{0:T(128)}, u32[]{:S(2)}) copy-start(f32[128]{0:T(128)} %copy-done.23) | copy-start | bytes 1540
  568.3 6.4 %copy-start.26 = (f32[128]{0:T(128)S(1)}, f32[128]{0:T(128)}, u32[]{:S(2)}) copy-start(f32[128]{0:T(128)} %copy-done.25) | copy-start | bytes 1540
Sparse Core Ops, SparseCore 0:
  11.8 68.3 all-gather.6
  82.6 56.2 all-gather.4
  140.8 147.6 all-gather.8
  292.0 88.2 reduce-scatter.1
  381.9 60.1 all-gather.10
where the time goes:
time: 584 us; the launch traced here: 582 us
  waiting for transfers between devices  382 us (65%)
  matrix products  80.1 us (14%)
  local copies, waits for them, and re-layouts  40.9 us (7%)
  starting transfers between devices  27.5 us (5%)
  blocking collectives  19.3 us (3%)
  other arithmetic  16.2 us (3%)
  between operations  13.7 us (2%)
    all_gather x1, waiting for transfers between devices, local(): lax.all_gather(qkv_weight, 'section', axis=0, tiled=True)  139 us
    reduce_scatter x1, waiting for transfers between devices, local(): lax.psum_scatter(lax.dot_general(pre_grad, fc1_weight, (((1,), (1,)), (()...  78.4 us
    all_gather x1, waiting for transfers between devices, local(): lax.all_gather(proj_weight, 'section', axis=0, tiled=True)  60.4 us
    all_gather x1, waiting for transfers between devices, local(): lax.all_gather(merged_grad, 'vit', axis=0, tiled=True)  54 us
    all_to_all x1, waiting for transfers between devices, local(): lax.all_to_all(outgoing, ('section', 'vit'), split_axis=0, concat_axis=0,...  24.7 us
    all_to_all x1, blocking collectives, local(): lax.all_to_all(head_result, 'vit', split_axis=3, concat_axis=1, tiled=True)  19.3 us
    all_gather x1, waiting for transfers between devices, local(): lax.all_gather(merge_in, 'vit', axis=0, tiled=True)  17.8 us
    all_to_all x1, starting transfers between devices, local(): lax.all_to_all(outgoing, ('section', 'vit'), split_axis=0, concat_axis=0,...  14.1 us
  transfers between devices with their start and end apart: 8, of which 7 were waited for; matrix products, arithmetic and copies ran while one was open for 7% of the time, Pallas kernels for 0%

commit v1 on v0

v1 whole, which is shorter than its diff:
```python
import functools

import jax
import jax.numpy as jnp
from jax import lax
from jax.experimental import pallas as pl
from jax.experimental.pallas import tpu as pltpu
from jax.sharding import PartitionSpec as P

HEADS = 16
LEVELS = 3
DV = 1152
DM = 4608
DL = 4096
HD = 72
SLOTS = 32
PATCHES = 128
WINDOW = 384
HIDDEN = 288
HALF = DM // 2
SCALE = HD**-0.5
norm_eps = 1e-06
MESH = pl.DeviceIdType.MESH
F32 = jnp.float32
BF16 = jnp.bfloat16

NN = (((1,), (0,)), ((), ()))
NT = (((1,), (1,)), ((), ()))


def dot(a, b, dims=NN):
    return lax.dot_general(a, b, dims, preferred_element_type=F32)


def normalize(values):
    row_mean = jnp.mean(values, axis=-1, keepdims=True)
    centered = values - row_mean
    variance = jnp.mean(centered * centered, axis=-1, keepdims=True)
    inverse = lax.rsqrt(variance + norm_eps)
    return (centered * inverse, inverse)


def normalize_back(upstream, normed_rows, inverse, gain):
    scaled = upstream * gain
    mean_scaled = jnp.mean(scaled, axis=-1, keepdims=True)
    mean_cross = jnp.mean(scaled * normed_rows, axis=-1, keepdims=True)
    return (scaled - mean_scaled - normed_rows * mean_cross) * inverse


def gelu_slope(pre_act):
    cumulative = 0.5 * (1.0 + lax.erf(pre_act * 0.7071067811865476))
    density = jnp.exp(-0.5 * pre_act * pre_act) * 0.3989422804014327
    return cumulative + pre_act * density


class Place:
    def __init__(self):
        self.s = lax.axis_index("section")
        v = lax.axis_index("vit")
        d = lax.axis_index("dp")
        self.x, self.y = lax.rem(v, 4), v // 4
        self.c, self.zl = lax.rem(d, 2), d // 2
        self.z = self.s * 2 + self.zl
        self.v = v

    def at(self, dx=0, dy=0):
        x, y = lax.rem(self.x + dx + 4, 4), lax.rem(self.y + dy + 4, 4)
        return {"section": self.s, "vit": y * 4 + x, "dp": self.zl * 2 + self.c}

    def up(self, dz):
        z = lax.rem(self.z + dz + 8, 8)
        return {"section": z // 2, "vit": self.v, "dp": lax.rem(z, 2) * 2 + self.c}

    def other_core(self):
        return {"section": self.s, "vit": self.v, "dp": self.zl * 2 + 1 - self.c}

    def along(self, dv):
        return {"section": self.s, "vit": lax.rem(self.v + dv + 16, 16), "dp": self.zl * 2 + self.c}


class Copies:
    def __init__(self, ssem, rsem):
        self.ssem, self.rsem, self.made = ssem, rsem, []

    def make(self, src, dst, device):
        k = len(self.made)
        copy = pltpu.make_async_remote_copy(
            src, dst, self.ssem.at[k], self.rsem.at[k], device_id=device, device_id_type=MESH
        )
        self.made.append(copy)
        return copy

    def drain(self):
        for copy in self.made:
            copy.wait_send()


class PlaneGather:
    def __init__(self, place, copies, buf, width, split):
        self.parts = []
        for axis in (0, 1):
            cols = pl.ds(0, split) if axis == 0 else pl.ds(split, width - split)

            def block(d1, d2, axis=axis):
                dx, dy = (d1, d2) if axis == 0 else (d2, d1)
                return lax.rem(place.y + dy + 4, 4) * 4 + lax.rem(place.x + dx + 4, 4)

            def first(d, axis=axis):
                return place.at(d, 0) if axis == 0 else place.at(0, d)

            def second(d, axis=axis):
                return place.at(0, d) if axis == 0 else place.at(d, 0)

            def send(d1, d2, rows, device, block=block, cols=cols):
                ref = buf.at[block(d1, d2), rows, cols]
                return copies.make(ref, ref, device)

            every, low, high = pl.ds(0, 32), pl.ds(0, 16), pl.ds(16, 16)
            part = {
                "s1p": send(0, 0, every, first(1)),
                "s1m": send(0, 0, every, first(-1)),
                "f1p": send(-1, 0, low, first(1)),
                "f1m": send(1, 0, high, first(-1)),
            }
            for d1 in (0, -1, 1, 2):
                part["s2p", d1] = send(d1, 0, every, second(1))
                part["s2m", d1] = send(d1, 0, every, second(-1))
                part["f2p", d1] = send(d1, -1, low, second(1))
                part["f2m", d1] = send(d1, 1, high, second(-1))
            self.parts.append(part)

    def start(self):
        for p in self.parts:
            for k in ("s1p", "s1m", ("s2p", 0), ("s2m", 0)):
                p[k].start()

    def near(self):
        for p in self.parts:
            p["s1p"].wait_recv()
            p["f1p"].start()
            p["s2p", -1].start()
            p["s2m", -1].start()
            p["s1m"].wait_recv()
            p["f1m"].start()
            p["s2p", 1].start()
            p["s2m", 1].start()

    def far(self):
        for p in self.parts:
            p["f1p"].wait_recv()
            p["f1m"].wait_recv()
            p["s2p", 2].start()
            p["s2m", 2].start()

    def pass_on(self, d1):
        for p in self.parts:
            p["s2p", d1].wait_recv()
            p["f2p", d1].start()
            p["s2m", d1].wait_recv()
            p["f2m", d1].start()

    def finish(self):
        for d1 in (0, -1, 1, 2):
            for p in self.parts:
                p["f2p", d1].wait_recv()
                p["f2m", d1].wait_recv()


class WeightGather:
    def __init__(self, place, copies, qkv, proj):
        s, c, zl = place.s, place.c, place.zl
        self.odd = zl == 1
        self.even = zl == 0
        chunks = [
            (qkv, 48, n * 48, 3456, 1792) for n in range(3)
        ] + [(proj, 144, 0, 1152, 640)]

        def piece(chunk, section, side):
            ref, rows, offset, width, split = chunk
            start = pl.multiple_of(lax.rem(section + 8, 4) * 288 + c * 144 + offset, 16)
            cols = {
                0: pl.ds(0, width), 1: pl.ds(0, split), 2: pl.ds(split, width - split)
            }[side]
            return ref.at[pl.ds(start, rows), cols]

        def make(chunk, section, side, device):
            ref = piece(chunk, section, side)
            return copies.make(ref, ref, device)

        right, left, core = place.up(1), place.up(-1), place.other_core()
        self.right, self.left = [], []
        for ch in chunks:
            self.right.append((
                make(ch, s - 1 + zl, 0, right),
                make(ch, s - 1, 0, core),
                make(ch, s - 2 + zl, 1, right),
                make(ch, s - 2, 1, core),
            ))
            self.left.append((
                make(ch, s + zl, 0, left),
                make(ch, s + 1, 0, core),
                make(ch, s + zl + 1, 2, left),
                make(ch, s + 2, 2, core),
            ))

    def start(self):
        @pl.when(self.odd)
        def _():
            for whole, *_ in self.right:
                whole.start()

        @pl.when(self.even)
        def _():
            for whole, *_ in self.left:
                whole.start()

    def whole(self, n):
        for lead, follow, side in ((self.odd, self.even, self.right), (self.even, self.odd, self.left)):
            whole, core, part, _ = side[n]
            whole.wait_recv()
            core.start()
            pl.when(follow)(whole.start)
            pl.when(lead)(part.start)

    def part(self, n):
        for follow, side in ((self.even, self.right), (self.odd, self.left)):
            _, _, part, core = side[n]
            part.wait_recv()
            core.start()
            pl.when(follow)(part.start)

    def finish(self):
        for side in (self.right, self.left):
            for _, core, _, core_part in side:
                core.wait_recv()
                core_part.wait_recv()


def body(
    grad, vit_in, vit_out, qkv_w, proj_w, fc1_w, fc2_w,
    section_weight, slot_pos, live_slot, id_row, id_col, live_row,
    ln_gain, ln_bias, merge_gain, merge_bias, fc1_bias,
    out_ref,
    xo, xin, rows_in, rows_grad, zin, zown, fc1, fc2, qkv, proj,
    h_out, r_out, h_in, r_in, wide, slope, hidden, pre_grad,
    ps, rb1, rb2, qs, rb3, merge_total, og,
    t32, heads, k_rows, v_rows, probs, o_cols, pg, strips, ssem, rsem, lsem,
):
    place = Place()
    s, x, y = place.s, place.x, place.y
    copies = Copies(ssem, rsem)

    near = [place.at(1, 0), place.at(-1, 0), place.at(2, 0), place.at(0, 1), place.at(0, -1), place.at(0, 2)]
    near += [place.up(1), place.up(-1), place.up(2), place.up(-2), place.up(4), place.other_core()]
    near += [place.along(1), place.along(-1)]
    barrier = pltpu.get_barrier_semaphore()
    for device in near:
        pl.semaphore_signal(barrier, inc=1, device_id=device, device_id_type=MESH)

    own_rows = pl.ds(pl.multiple_of(s * 288, 16), 288)
    group_rows = pl.ds(pl.multiple_of(s * 32, 32), 32)
    local = [
        pltpu.make_async_copy(src, dst, lsem.at[k])
        for k, (src, dst) in enumerate((
            (vit_out, xo),
            (grad.at[group_rows], zown),
            (vit_in, xin.at[1]),
            (fc1_w, fc1),
            (qkv_w, qkv.at[own_rows]),
            (proj_w, proj.at[own_rows]),
            (fc2_w, fc2),
        ))
    ]
    for copy in local:
        copy.start()

    me = place.v
    local[0].wait()
    h, r = normalize(xo[...].astype(F32))
    h_out[...] = h
    r_out[...] = r
    value = h * merge_gain[...] + merge_bias[...]
    for t in range(9):
        strips[t] = value[:, 128 * t : 128 * t + 128]
    for p in range(4):
        for t in range(9):
            strip = strips[t, pl.ds(p, SLOTS, stride=4), :]
            rows_in[me, :, pl.ds(DV * p + 128 * t, 128)] = strip.astype(BF16)

    pl.semaphore_wait(barrier, len(near))

    z_copies = []
    for d in (1, 2, 3):
        rows = pl.ds(pl.multiple_of(lax.rem(s + d, 4) * 32, 32), 32)
        z_copies.append(copies.make(grad.at[rows], zin.at[d - 1], place.up(2 * d)))
    for copy in (z_copies[0], z_copies[2], z_copies[1]):
        copy.start()
    gather_in = PlaneGather(place, copies, rows_in, DM, HALF)
    gather_in.start()
    halo_in = [
        copies.make(vit_in, xin.at[0], place.along(1)),
        copies.make(vit_in, xin.at[2], place.along(-1)),
    ]
    for copy in halo_in:
        copy.start()
    gather_grad = PlaneGather(place, copies, rows_grad, DL, DL // 2)
    weights = WeightGather(place, copies, qkv, proj)

    gather_in.near()
    gather_in.pass_on(0)
    gather_in.far()

    for copy in z_copies:
        copy.wait_recv()
    for copy in (local[1], local[4], local[5]):
        copy.wait()
    weights.start()

    @pl.loop(0, 4)
    def _(i):
        cols = pl.ds(pl.multiple_of(i * 1024, 128), 1024)
        total = section_weight[0, s] * zown[:, cols].astype(F32)
        for d in (1, 2, 3):
            total += section_weight[0, lax.rem(s - d + 4, 4)] * zin[d - 1, :, cols].astype(F32)
        rows_grad[me, :, cols] = total.astype(BF16)

    gather_grad.start()
    gather_in.pass_on(-1)
    gather_in.pass_on(1)
    gather_in.pass_on(2)
    weights.whole(0)
    gather_grad.near()
    gather_in.finish()
    local[3].wait()

    def fill_slope(lo, hi):
        @pl.loop(lo, hi)
        def _(i):
            block = rows_in[pl.ds(i * 4, 4)].reshape(128, DM)
            rows = pl.ds(pl.multiple_of(i * 128, 128), 128)
            slope[rows, :] = gelu_slope(dot(block, fc1[...], NT) + fc1_bias[...])

    fill_slope(0, 2)
    gather_grad.pass_on(0)
    gather_grad.far()
    fill_slope(2, 4)
    weights.whole(1)
    gather_grad.pass_on(-1)
    gather_grad.pass_on(1)
    weights.whole(2)
    gather_grad.pass_on(2)
    local[6].wait()
    gather_grad.finish()

    @pl.loop(0, 4)
    def _(i):
        block = rows_grad[pl.ds(i * 4, 4)].reshape(128, DL)
        rows = pl.ds(pl.multiple_of(i * 128, 128), 128)
        hidden[rows, :] = dot(block, fc2[...], NT)

    value = hidden[...]
    high = value.astype(BF16)
    low = (value - high.astype(F32)).astype(BF16)
    for i in range(4):
        slots = lax.broadcasted_iota(jnp.int32, (128, 512), 0) + 128 * i
        chosen = jnp.where(slots == slot_pos[...], 1.0, 0.0).astype(BF16)
        placed = dot(chosen, high) + dot(chosen, low)
        rows = pl.ds(128 * i, 128)
        live = live_slot[rows, :] > 0.0
        block = jnp.where(live, placed, 0.0) * slope[rows, :]
        pre_grad[pl.ds(4 * i, 4)] = block.astype(BF16).reshape(4, SLOTS, HIDDEN)

    def token(part, d1, d2):
        dx, dy = (d1, d2) if part == 0 else (d2, d1)
        return lax.rem(y + dy, 4) * 4 + lax.rem(x + dx, 4)

    def first(part, d):
        return place.at(d, 0) if part == 0 else place.at(0, d)

    def second(part, d):
        return place.at(0, d) if part == 0 else place.at(d, 0)

    def product(part, d1):
        block = jnp.concatenate([pre_grad[token(part, d1, d2)] for d2 in range(4)], axis=0)

        @pl.loop(0, 6)
        def _(i):
            start = pl.multiple_of(i * 384, 128)
            cols = pl.ds(pl.multiple_of(start + part * HALF, 128), 384)
            term = dot(block, fc1[:, cols]).astype(BF16).reshape(4, SLOTS, 384)
            ps[part, d1, :, :, pl.ds(start, 384)] = term

    def scatter(part):
        low, high = pl.ds(0, 2), pl.ds(2, 2)
        near1, near2 = first(part, 1), first(part, -1)
        return {
            "1p": copies.make(ps.at[part, 2, low], rb1.at[part, 0], near1),
            "1m": copies.make(ps.at[part, 2, high], rb1.at[part, 1], near2),
            "2p": [copies.make(ps.at[part, 1, k], rb2.at[part, 0, k], near1) for k in range(4)],
            "2m": [copies.make(ps.at[part, 3, k], rb2.at[part, 1, k], near2) for k in range(4)],
            "3": [copies.make(qs.at[part, k - 1], rb3.at[part, k - 1], second(part, k)) for k in (1, 2, 3)],
        }

    sums = [scatter(0), scatter(1)]
    for part in (0, 1):
        product(part, 2)
        sums[part]["1p"].start()
        sums[part]["1m"].start()
    for part in (0, 1):
        product(part, 1)
        for k in (2, 3):
            sums[part]["2p"][k].start()
        product(part, 3)
        for k in (0, 1):
            sums[part]["2m"][k].start()

    def add(part, d1, k, got):
        ps[part, d1, k] = (ps[part, d1, k].astype(F32) + got[...].astype(F32)).astype(BF16)

    for part in (0, 1):
        sums[part]["1p"].wait_recv()
        for k in (1, 0):
            add(part, 1, k, rb1.at[part, 0, k])
            sums[part]["2p"][k].start()
        sums[part]["1m"].wait_recv()
        for k in (3, 2):
            add(part, 3, k, rb1.at[part, 1, k - 2])
            sums[part]["2m"][k].start()
    for part in (0, 1):
        product(part, 0)

    weights.whole(3)
    for n in range(4):
        weights.part(n)

    for k in (2, 3, 1, 0):
        for part in (0, 1):
            sums[part]["2p"][k].wait_recv()
            sums[part]["2m"][k].wait_recv()
            total = (
                ps[part, 0, k].astype(F32)
                + rb2[part, 0, k].astype(F32)
                + rb2[part, 1, k].astype(F32)
            )
            if k:
                qs[part, k - 1] = total.astype(BF16)
                sums[part]["3"][k - 1].start()
            else:
                merge_total[:, pl.ds(part * HALF, HALF)] = total

    for copy in halo_in:
        copy.wait_recv()
    local[2].wait()
    for w in range(3):
        h, r = normalize(xin[w].astype(F32))
        if w == 1:
            h_in[...] = h
            r_in[...] = r
        xin[w] = (h * ln_gain[...] + ln_bias[...]).astype(BF16)
    weights.finish()
    for j in range(3):
        for i in range(3):
            block = dot(xin[...].reshape(WINDOW, DV), qkv[:, pl.ds(j * DV + i * 384, 384)])
            t32[pl.ds(i * 384, 384), :] = block.T

        @pl.loop(0, HEADS)
        def _(n):
            cols = t32[pl.ds(pl.multiple_of(n * HD, 8), HD), :]
            heads[j * HEADS + n] = cols.astype(BF16)
            if j == 1:
                k_rows[n] = cols.T.astype(BF16)
            if j == 2:
                v_rows[n] = cols.T.astype(BF16)

    @pl.loop(0, HEADS)
    def _(n):
        scores = dot(k_rows[n], heads[n]) * SCALE
        allowed = id_col[...] == id_row[...]
        exponent = jnp.where(allowed, jnp.exp(jnp.where(allowed, scores, 0.0)), 0.0)
        denominator = jnp.sum(exponent, axis=0, keepdims=True) + 1.0 - live_row[...]
        weight = (exponent / denominator).astype(BF16)
        probs[n] = weight
        o_cols[n] = dot(heads[2 * HEADS + n], weight)

    for part in (0, 1):
        cols = pl.ds(part * HALF, HALF)
        for k in (2, 3, 1):
            sums[part]["3"][k - 1].wait_recv()
            merge_total[:, cols] += rb3[part, k - 1].astype(F32)
    for p in range(4):
        for t in range(9):
            strips[t, pl.ds(p, SLOTS, stride=4), :] = merge_total[:, pl.ds(DV * p + 128 * t, 128)]
    for t in range(9):
        wide[:, pl.ds(128 * t, 128)] = strips[t]
    og[1] = normalize_back(wide[...], h_out[...], r_out[...], merge_gain[...]).astype(BF16)
    halo_out = [
        copies.make(og.at[1], og.at[0], place.along(1)),
        copies.make(og.at[1], og.at[2], place.along(-1)),
    ]
    for copy in halo_out:
        copy.start()

    def project_back(w):
        for i in range(3):
            t32[pl.ds(i * 384, 384), pl.ds(w * PATCHES, PATCHES)] = dot(
                proj[pl.ds(i * 384, 384), :], og[w], NT
            )

    project_back(1)
    for w, copy in ((0, halo_out[0]), (2, halo_out[1])):
        copy.wait_recv()
        project_back(w)

    own = pl.ds(PATCHES, PATCHES)

    @pl.loop(0, HEADS)
    def _(n):
        start = pl.multiple_of(n * HD, 8)
        upstream = t32[pl.ds(start, HD), :].astype(BF16)
        delta = jnp.sum(upstream.astype(F32) * o_cols[n], axis=0, keepdims=True)
        prob1 = dot(v_rows[n], upstream[:, PATCHES : 2 * PATCHES])
        weight1 = probs[n, :, own].astype(F32)
        score1 = weight1 * (prob1 - delta[:, PATCHES : 2 * PATCHES]) * SCALE
        pg[pl.ds(start, HD), :] = dot(heads[HEADS + n], score1.astype(BF16))
        prob2 = dot(v_rows[n, own, :], upstream)
        weight2 = probs[n, own, :]
        score2 = (weight2.astype(F32) * (prob2 - delta) * SCALE).astype(BF16)
        pg[pl.ds(pl.multiple_of(start + DV, 8), HD), :] = dot(heads[n], score2, NT)
        pg[pl.ds(pl.multiple_of(start + 2 * DV, 8), HD), :] = dot(upstream, weight2, NT)

    projected_grad = pg[...].astype(BF16)
    for i in range(3):
        block = dot(qkv[pl.ds(i * 384, 384), :], projected_grad)
        wide[:, pl.ds(i * 384, 384)] = block.T
    out_ref[...] = (
        og[1].astype(F32) + normalize_back(wide[...], h_in[...], r_in[...], ln_gain[...])
    ).astype(BF16)
    copies.drain()


N_COPIES = 3 + 40 + 2 + 40 + 32 + 26 + 2


def local(
    grad_llm,
    vis_slot,
    image_rows,
    section_layer,
    vit_in,
    vit_out,
    ln_gain,
    ln_bias,
    qkv_weight,
    proj_weight,
    merge_gain,
    merge_bias,
    fc1_weight,
    fc1_bias,
    fc2_weight,
):
    s = lax.axis_index("section")
    v = lax.axis_index("vit")
    section_weight = jnp.where(
        section_layer < LEVELS, (section_layer + 1).astype(F32) / LEVELS, 0.0
    ).reshape(1, 4)
    counts = lax.dynamic_index_in_dim(image_rows, s, 0, keepdims=True)
    order = jnp.arange(16, dtype=jnp.int32)
    ends = jnp.sum(jnp.where(order[None, :] <= order[:, None], counts, 0), axis=1)
    total = jnp.sum(counts)
    slot_pos = lax.dynamic_slice_in_dim(vis_slot, s * 32, 32, 1).reshape(1, 512) - s * 512
    live_slot = (jnp.arange(512, dtype=jnp.int32) < total).astype(F32)[:, None]
    patch = v * PATCHES - PATCHES + jnp.arange(WINDOW, dtype=jnp.int32)
    slot = patch >> 2
    image = jnp.sum((slot[:, None] >= ends[None, :]).astype(jnp.int32), axis=1)
    live = (patch >= 0) & (slot < total)
    id_row = jnp.where(live, image, -1)[None, :]
    id_col = jnp.where(live, image, -2)[:, None]
    live_row = live.astype(F32)[None, :]

    anywhere = pl.BlockSpec(memory_space=pl.ANY)
    vmem = pl.BlockSpec(memory_space=pltpu.VMEM)
    smem = pl.BlockSpec(memory_space=pltpu.SMEM)

    def scratch(shape, dtype=BF16):
        return pltpu.VMEM(shape, dtype)

    return pl.pallas_call(
        body,
        out_shape=jax.ShapeDtypeStruct((PATCHES, DV), BF16),
        in_specs=[anywhere] * 7 + [smem] + [vmem] * 10,
        out_specs=vmem,
        scratch_shapes=[
            scratch((PATCHES, DV)),
            scratch((3, PATCHES, DV)),
            scratch((16, SLOTS, DM)),
            scratch((16, SLOTS, DL)),
            scratch((3, 32, DL)),
            scratch((32, DL)),
            scratch((HIDDEN, DM)),
            scratch((HIDDEN, DL)),
            scratch((DV, 3 * DV)),
            scratch((DV, DV)),
            scratch((PATCHES, DV), F32),
            scratch((PATCHES, 1), F32),
            scratch((PATCHES, DV), F32),
            scratch((PATCHES, 1), F32),
            scratch((PATCHES, DV), F32),
            scratch((512, HIDDEN), F32),
            scratch((512, HIDDEN), F32),
            scratch((16, SLOTS, HIDDEN)),
            scratch((2, 4, 4, SLOTS, HALF)),
            scratch((2, 2, 2, SLOTS, HALF)),
            scratch((2, 2, 4, SLOTS, HALF)),
            scratch((2, 3, SLOTS, HALF)),
            scratch((2, 3, SLOTS, HALF)),
            scratch((SLOTS, DM), F32),
            scratch((3, PATCHES, DV)),
            scratch((DV, WINDOW), F32),
            scratch((3 * HEADS, HD, WINDOW)),
            scratch((HEADS, WINDOW, HD)),
            scratch((HEADS, WINDOW, HD)),
            scratch((HEADS, WINDOW, WINDOW)),
            scratch((HEADS, HD, WINDOW), F32),
            scratch((3 * DV, PATCHES), F32),
            scratch((9, PATCHES, 128), F32),
            pltpu.SemaphoreType.DMA((N_COPIES,)),
            pltpu.SemaphoreType.DMA((N_COPIES,)),
            pltpu.SemaphoreType.DMA((7,)),
        ],
        compiler_params=pltpu.CompilerParams(
            collective_id=0, has_side_effects=True, vmem_limit_bytes=60 * 2**20
        ),
        name="merger_and_attention",
    )(
        grad_llm.reshape(grad_llm.shape[1:]),
        vit_in,
        vit_out,
        qkv_weight,
        proj_weight,
        fc1_weight.T,
        fc2_weight,
        section_weight,
        slot_pos,
        live_slot,
        id_row,
        id_col,
        live_row,
        ln_gain.reshape(1, DV),
        ln_bias.reshape(1, DV),
        merge_gain.reshape(1, DV),
        merge_bias.reshape(1, DV),
        fc1_bias.reshape(1, HIDDEN),
    )


def solution(mesh):
    placed = (
        P("section", ("dp", "vit"), None),
        P("dp", None),
        P("dp", None),
        P(),
        P(("dp", "section", "vit"), None),
        P(("dp", "section", "vit"), None),
        P(),
        P(),
        P("section", None),
        P("section", None),
        P(),
        P(),
        P(None, "vit"),
        P("vit"),
        P("vit", None),
    )
    return jax.shard_map(
        local,
        mesh=mesh,
        in_specs=placed,
        out_specs=P(("dp", "section", "vit"), None),
        check_vma=False,
    )
```

time: 584 us -> 233 us (0.40)
  waiting for transfers between devices: 382 us -> 0 us
  Pallas kernels: 0 us -> 211 us
  matrix products: 80.1 us -> 0 us
  local copies, waits for them, and re-layouts: 40.9 us -> 8.78 us
  starting transfers between devices: 27.5 us -> 0 us
  blocking collectives: 19.3 us -> 0 us
  between operations: 13.7 us -> 0.02 us
  other arithmetic: 16.2 us -> 9.04 us
    all_gather x4 -> x0, waiting for transfers between devices: 271 us -> none  [the longest x1 139 us: local(): lax.all_gather(qkv_weight, 'section', axis=0, tiled=True)]
    pallas_call x0 -> x1, Pallas kernels: none -> 211 us  [local(): pl.pallas_call(body, out_shape=jax.ShapeDtypeStruct((PATCHES, DV), BF16),...]
    dot_general x25 -> x0, matrix products: 80.1 us -> none  [the longest x4 13.8 us: step(): lax.dot_general(query_block, key_cols, contract_first, preferred_element_...]
    reduce_scatter x1 -> x0, waiting for transfers between devices: 78.4 us -> none  [local(): lax.psum_scatter(lax.dot_general(pre_grad, fc1_weight, (((1,), (1,)), (()...]
    all_to_all x3 -> x0, waiting for transfers between devices: 31.2 us -> none  [the longest x1 24.7 us: local(): lax.all_to_all(outgoing, ('section', 'vit'), split_axis=0, concat_axis=0,...]
    all_to_all x3 -> x0, starting transfers between devices: 27.3 us -> none  [the longest x1 14.1 us: local(): lax.all_to_all(outgoing, ('section', 'vit'), split_axis=0, concat_axis=0,...]
    all_to_all x1 -> x0, blocking collectives: 19.3 us -> none  [local(): lax.all_to_all(head_result, 'vit', split_axis=3, concat_axis=1, tiled=True)]
    while x20 -> x0, local copies, waits for them, and re-layouts: 7.97 us -> none
  transfers between devices with their start and end apart: 8 -> 0, of which waited for: 7 -> 0; matrix products, arithmetic and copies ran while one was open for 7% -> 0% of each run, Pallas kernels for 0% -> 0%
where the time goes in v1:
time: 233 us; the launch traced here: 229 us
  Pallas kernels  211 us (91%)
  other arithmetic  9.04 us (4%)
  local copies, waits for them, and re-layouts  8.78 us (4%)
    pallas_call x1, Pallas kernels, local(): pl.pallas_call(body, out_shape=jax.ShapeDtypeStruct((PATCHES, DV), BF16),...  211 us

profile of v1, /device:TPU:64, one launch (start us, length us, event | category | flops | bytes accessed | tf_op | source)
XLA Modules:
  0.0 229.1 jit_solution(13783688285382898243)
XLA Ops:
  0.0 1.2 fusion.4.section_weight
  1.2 1.4 fusion.5
  2.6 0.1 select_reduce_fusion
  2.8 1.3 fusion.3.live_row
  4.0 1.3 reshape.111.fc1_bias
  5.3 0.1 convert_reduce_fusion
  5.4 1.2 reshape_select_fusion.1.id_row
  6.6 1.3 reshape.107.ln_gain
  7.9 1.3 reshape.108.ln_bias
  9.2 1.3 reshape.109.merge_gain
  10.5 1.3 reshape.110.merge_bias
  11.8 0.8 dynamic-slice_subtract_fusion
  12.6 0.7 sub.13.slot_pos
  13.2 1.5 reshape_select_fusion.id_col
  14.7 1.4 fusion.live_slot
  16.1 211.2 %merger_and_attention.1 = bf16[128,1152]{1,0:T(8,128)(2,1)} custom-call(bf16[128,4096]{1,0:T(8,128)(2,1)} %bitcast.7, bf16[128,1152]{1,0:T(8,128)(2,1)} %vit_in.1, bf16[128,1152]{1,0:T(8,128)(2,1)} %vit_out.1, bf16[288,3456]{1,0:T(8,128)(2,1)} %qkv_w.1, bf16[288,1152]{1,0:T(8,128)(2,1)} %proj_w.1, bf16[288,4608]{1,0:T(8,128)(2,1)} %bitcast.6, ...), custom_call_target="tpu_custom_call" | custom-call | tf_op jit(solution)/shard_map/merger_and_attention/pallas_call | solution.py:587
  227.4 1.7 copy.19
  (1 shorter events, 0.0 us)

commit v2 on v1

--- a/solution.py
+++ b/solution.py
@@ -80,14 +80,16 @@
 
 class Copies:
     def __init__(self, ssem, rsem):
-        self.ssem, self.rsem, self.made = ssem, rsem, []
-
-    def make(self, src, dst, device):
-        k = len(self.made)
+        self.ssem, self.rsem, self.made, self.count = ssem, rsem, [], 0
+
+    def make(self, src, dst, device, drained=True):
+        k = self.count
+        self.count += 1
         copy = pltpu.make_async_remote_copy(
             src, dst, self.ssem.at[k], self.rsem.at[k], device_id=device, device_id_type=MESH
         )
-        self.made.append(copy)
+        if drained:
+            self.made.append(copy)
         return copy
 
     def drain(self):
@@ -183,68 +185,108 @@
             }[side]
             return ref.at[pl.ds(start, rows), cols]
 
-        def make(chunk, section, side, device):
+        def make(chunk, section, side, device, drained=True):
             ref = piece(chunk, section, side)
-            return copies.make(ref, ref, device)
+            return copies.make(ref, ref, device, drained)
 
         right, left, core = place.up(1), place.up(-1), place.other_core()
         self.right, self.left = [], []
         for ch in chunks:
             self.right.append((
-                make(ch, s - 1 + zl, 0, right),
+                make(ch, s - 1 + zl, 0, right, False),
                 make(ch, s - 1, 0, core),
                 make(ch, s - 2 + zl, 1, right),
                 make(ch, s - 2, 1, core),
             ))
             self.left.append((
-                make(ch, s + zl, 0, left),
+                make(ch, s + zl, 0, left, False),
                 make(ch, s + 1, 0, core),
                 make(ch, s + zl + 1, 2, left),
                 make(ch, s + 2, 2, core),
             ))
 
+    def each(self):
+        return ((self.odd, self.even, self.right), (self.even, self.odd, self.left))
+
     def start(self):
-        @pl.when(self.odd)
-        def _():
-            for whole, *_ in self.right:
+        for lead, _, side in self.each():
+            pl.when(lead)(side[0][0].start)
+
+    def follow_whole(self, n):
+        for lead, follow, side in self.each():
+            whole, core, _, _ = side[n]
+            if n < 3:
+
+                @pl.when(lead)
+                def _():
+                    whole.wait_send()
+                    side[n + 1][0].start()
+
+            @pl.when(follow)
+            def _():
+                whole.wait_recv()
+                core.start()
                 whole.start()
 
-        @pl.when(self.even)
-        def _():
-            for whole, *_ in self.left:
-                whole.start()
-
-    def whole(self, n):
-        for lead, follow, side in ((self.odd, self.even, self.right), (self.even, self.odd, self.left)):
+    def lead_whole(self, n):
+        for lead, _, side in self.each():
             whole, core, part, _ = side[n]
-            whole.wait_recv()
-            core.start()
-            pl.when(follow)(whole.start)
-            pl.when(lead)(part.start)
-
-    def part(self, n):
-        for follow, side in ((self.even, self.right), (self.odd, self.left)):
+
+            @pl.when(lead)
+            def _():
+                whole.wait_recv()
+                core.start()
+                part.start()
+
+    def follow_part(self, n):
+        for _, follow, side in self.each():
             _, _, part, core = side[n]
-            part.wait_recv()
-            core.start()
-            pl.when(follow)(part.start)
-
-    def finish(self):
+
+            @pl.when(follow)
+            def _():
+                part.wait_recv()
+                core.start()
+                part.start()
+
+    def lead_part(self, n):
+        for lead, _, side in self.each():
+            _, _, part, core = side[n]
+
+            @pl.when(lead)
+            def _():
+                part.wait_recv()
+                core.start()
+
+    def step(self, k):
+        for n, act in (
+            (k, self.follow_whole), (k - 1, self.lead_whole), (k - 2, self.follow_part), (k - 3, self.lead_part)
+        ):
+            if 0 <= n < 4:
+                act(n)
+
+    def finish(self, pieces):
         for side in (self.right, self.left):
-            for _, core, _, core_part in side:
-                core.wait_recv()
-                core_part.wait_recv()
+            for n in pieces:
+                side[n][1].wait_recv()
+                side[n][3].wait_recv()
+
+    def drain(self):
+        for _, follow, side in self.each():
+            for n in range(3):
+                pl.when(follow)(side[n][0].wait_send)
+            side[3][0].wait_send()
 
 
 def body(
     grad, vit_in, vit_out, qkv_w, proj_w, fc1_w, fc2_w,
-    section_weight, slot_pos, live_slot, id_row, id_col, live_row,
-    ln_gain, ln_bias, merge_gain, merge_bias, fc1_bias,
+    ln_gain_h, ln_bias_h, merge_gain_h, merge_bias_h, fc1_bias_h, vis_slot_h,
+    image_rows, section_layer,
     out_ref,
     xo, xin, rows_in, rows_grad, zin, zown, fc1, fc2, qkv, proj,
     h_out, r_out, h_in, r_in, wide, slope, hidden, pre_grad,
     ps, rb1, rb2, qs, rb3, merge_total, og,
-    t32, heads, k_rows, v_rows, probs, o_cols, pg, strips, ssem, rsem, lsem,
+    t32, heads, k_rows, v_rows, probs, o_cols, pg, strips,
+    ln_gain_v, ln_bias_v, merge_gain_v, merge_bias_v, fc1_bias_v, vis_slot, ssem, rsem, lsem,
 ):
     place = Place()
     s, x, y = place.s, place.x, place.y
@@ -269,17 +311,26 @@
             (qkv_w, qkv.at[own_rows]),
             (proj_w, proj.at[own_rows]),
             (fc2_w, fc2),
+            (merge_gain_h, merge_gain_v),
+            (merge_bias_h, merge_bias_v),
+            (ln_gain_h, ln_gain_v),
+            (ln_bias_h, ln_bias_v),
+            (fc1_bias_h, fc1_bias_v),
+            (vis_slot_h, vis_slot),
         ))
     ]
-    for copy in local:
-        copy.start()
+    for k in (0, 7, 8, 1, 4, 5, 3, 6, 2, 9, 10, 11, 12):
+        local[k].start()
 
     me = place.v
-    local[0].wait()
+    for k in (0, 7, 8):
+        local[k].wait()
+    merge_gain = merge_gain_v[...].reshape(1, DV)
+    merge_bias = merge_bias_v[...].reshape(1, DV)
     h, r = normalize(xo[...].astype(F32))
     h_out[...] = h
     r_out[...] = r
-    value = h * merge_gain[...] + merge_bias[...]
+    value = h * merge_gain + merge_bias
     for t in range(9):
         strips[t] = value[:, 128 * t : 128 * t + 128]
     for p in range(4):
@@ -301,55 +352,66 @@
         copies.make(vit_in, xin.at[0], place.along(1)),
         copies.make(vit_in, xin.at[2], place.along(-1)),
     ]
-    for copy in halo_in:
-        copy.start()
     gather_grad = PlaneGather(place, copies, rows_grad, DL, DL // 2)
     weights = WeightGather(place, copies, qkv, proj)
+    for k in (4, 5):
+        local[k].wait()
+    weights.start()
 
     gather_in.near()
     gather_in.pass_on(0)
     gather_in.far()
-
+    gather_in.pass_on(-1)
+    gather_in.pass_on(1)
+    weights.step(0)
+    gather_in.pass_on(2)
+    local[1].wait()
     for copy in z_copies:
         copy.wait_recv()
-    for copy in (local[1], local[4], local[5]):
-        copy.wait()
-    weights.start()
+
+    level = [section_layer[lax.rem(s + 4 - d, 4)] for d in range(4)]
+    level = [
+        jnp.where(n == 0, 1 / 3, jnp.where(n == 1, 2 / 3, jnp.where(n == 2, 1.0, 0.0))).astype(F32)
+        for n in level
+    ]
 
     @pl.loop(0, 4)
     def _(i):
         cols = pl.ds(pl.multiple_of(i * 1024, 128), 1024)
-        total = section_weight[0, s] * zown[:, cols].astype(F32)
+        total = level[0] * zown[:, cols].astype(F32)
         for d in (1, 2, 3):
-            total += section_weight[0, lax.rem(s - d + 4, 4)] * zin[d - 1, :, cols].astype(F32)
+            total += level[d] * zin[d - 1, :, cols].astype(F32)
         rows_grad[me, :, cols] = total.astype(BF16)
 
     gather_grad.start()
-    gather_in.pass_on(-1)
-    gather_in.pass_on(1)
-    gather_in.pass_on(2)
-    weights.whole(0)
-    gather_grad.near()
+    for copy in halo_in:
+        copy.start()
+    weights.step(1)
     gather_in.finish()
-    local[3].wait()
+    for k in (3, 11):
+        local[k].wait()
+    fc1_bias = fc1_bias_v[...].reshape(1, HIDDEN)
 
     def fill_slope(lo, hi):
         @pl.loop(lo, hi)
         def _(i):
             block = rows_in[pl.ds(i * 4, 4)].reshape(128, DM)
             rows = pl.ds(pl.multiple_of(i * 128, 128), 128)
-            slope[rows, :] = gelu_slope(dot(block, fc1[...], NT) + fc1_bias[...])
-
+            slope[rows, :] = gelu_slope(dot(block, fc1[...], NT) + fc1_bias)
+
+    gather_grad.near()
     fill_slope(0, 2)
+    weights.step(2)
     gather_grad.pass_on(0)
     gather_grad.far()
     fill_slope(2, 4)
-    weights.whole(1)
+    weights.step(3)
     gather_grad.pass_on(-1)
     gather_grad.pass_on(1)
-    weights.whole(2)
+    weights.step(4)
     gather_grad.pass_on(2)
-    local[6].wait()
+    for k in (2, 6, 9, 10, 12):
+        local[k].wait()
     gather_grad.finish()
 
     @pl.loop(0, 4)
@@ -358,16 +420,35 @@
         rows = pl.ds(pl.multiple_of(i * 128, 128), 128)
         hidden[rows, :] = dot(block, fc2[...], NT)
 
+
+    weights.step(5)
+
+    ends = []
+    for k in range(16):
+        count = image_rows[s, k]
+        ends.append(count if k == 0 else ends[-1] + count)
+    total_slots = ends[-1]
+
+    shifted = [pltpu.roll(vis_slot[...], lax.rem(32 * q + 128 - 32 * s, 128), 1) for q in range(4)]
+    quarter = lax.broadcasted_iota(jnp.int32, (1, 128), 1) // 32
+    positions = []
+    for t in range(4):
+        position = shifted[0][4 * t : 4 * t + 1, :]
+        for q in (1, 2, 3):
+            position = jnp.where(quarter == q, shifted[q][4 * t + q : 4 * t + q + 1, :], position)
+        positions.append(position - 512 * s)
     value = hidden[...]
     high = value.astype(BF16)
     low = (value - high.astype(F32)).astype(BF16)
     for i in range(4):
-        slots = lax.broadcasted_iota(jnp.int32, (128, 512), 0) + 128 * i
-        chosen = jnp.where(slots == slot_pos[...], 1.0, 0.0).astype(BF16)
-        placed = dot(chosen, high) + dot(chosen, low)
-        rows = pl.ds(128 * i, 128)
-        live = live_slot[rows, :] > 0.0
-        block = jnp.where(live, placed, 0.0) * slope[rows, :]
+        slots = lax.broadcasted_iota(jnp.int32, (128, 128), 0) + 128 * i
+        placed = jnp.zeros((128, HIDDEN), F32)
+        for t in range(4):
+            chosen = jnp.where(slots == positions[t], 1.0, 0.0).astype(BF16)
+            from_rows = slice(128 * t, 128 * t + 128)
+            placed += dot(chosen, high[from_rows]) + dot(chosen, low[from_rows])
+        live = lax.broadcasted_iota(jnp.int32, (128, HIDDEN), 0) + 128 * i < total_slots
+        block = jnp.where(live, placed, 0.0) * slope[pl.ds(128 * i, 128), :]
         pre_grad[pl.ds(4 * i, 4)] = block.astype(BF16).reshape(4, SLOTS, HIDDEN)
 
     def token(part, d1, d2):
@@ -429,10 +510,35 @@
     for part in (0, 1):
         product(part, 0)
 
-    weights.whole(3)
-    for n in range(4):
-        weights.part(n)
-
+    weights.step(6)
+    for copy in halo_in:
+        copy.wait_recv()
+    ln_gain = ln_gain_v[...].reshape(1, DV)
+    ln_bias = ln_bias_v[...].reshape(1, DV)
+
+    for w in range(3):
+        h, r = normalize(xin[w].astype(F32))
+        if w == 1:
+            h_in[...] = h
+            r_in[...] = r
+        xin[w] = (h * ln_gain + ln_bias).astype(BF16)
+
+    def attend(j):
+        for i in range(3):
+            block = dot(xin[...].reshape(WINDOW, DV), qkv[:, pl.ds(j * DV + i * 384, 384)])
+            t32[pl.ds(i * 384, 384), :] = block.T
+
+        @pl.loop(0, HEADS, unroll=2)
+        def _(n):
+            cols = t32[pl.ds(pl.multiple_of(n * HD, 8), HD), :]
+            heads[j * HEADS + n] = cols.astype(BF16)
+            if j == 1:
+                k_rows[n] = cols.T.astype(BF16)
+            if j == 2:
+                v_rows[n] = cols.T.astype(BF16)
+
+    weights.finish((0, 1, 2))
+    attend(0)
     for k in (2, 3, 1, 0):
         for part in (0, 1):
             sums[part]["2p"][k].wait_recv()
@@ -447,37 +553,29 @@
                 sums[part]["3"][k - 1].start()
             else:
                 merge_total[:, pl.ds(part * HALF, HALF)] = total
-
-    for copy in halo_in:
-        copy.wait_recv()
-    local[2].wait()
-    for w in range(3):
-        h, r = normalize(xin[w].astype(F32))
-        if w == 1:
-            h_in[...] = h
-            r_in[...] = r
-        xin[w] = (h * ln_gain[...] + ln_bias[...]).astype(BF16)
-    weights.finish()
-    for j in range(3):
-        for i in range(3):
-            block = dot(xin[...].reshape(WINDOW, DV), qkv[:, pl.ds(j * DV + i * 384, 384)])
-            t32[pl.ds(i * 384, 384), :] = block.T
-
-        @pl.loop(0, HEADS)
-        def _(n):
-            cols = t32[pl.ds(pl.multiple_of(n * HD, 8), HD), :]
-            heads[j * HEADS + n] = cols.astype(BF16)
-            if j == 1:
-                k_rows[n] = cols.T.astype(BF16)
-            if j == 2:
-                v_rows[n] = cols.T.astype(BF16)
-
-    @pl.loop(0, HEADS)
+    attend(1)
+    attend(2)
+
+    def image_of(axis):
+        shape = (1, WINDOW) if axis else (WINDOW, 1)
+        patch = lax.broadcasted_iota(jnp.int32, shape, axis) + (place.v * PATCHES - PATCHES)
+        slot = patch >> 2
+        image = jnp.zeros(shape, jnp.int32)
+        for end in ends:
+            image += jnp.where(slot >= end, 1, 0)
+        live = (patch >= 0) & (slot < total_slots)
+        return jnp.where(live, image, axis - 2), live
+
+    id_row, live_row = image_of(1)
+    id_col, _ = image_of(0)
+    dead_row = jnp.where(live_row, 0.0, 1.0)
+
+    @pl.loop(0, HEADS, unroll=2)
     def _(n):
         scores = dot(k_rows[n], heads[n]) * SCALE
-        allowed = id_col[...] == id_row[...]
+        allowed = id_col == id_row
         exponent = jnp.where(allowed, jnp.exp(jnp.where(allowed, scores, 0.0)), 0.0)
-        denominator = jnp.sum(exponent, axis=0, keepdims=True) + 1.0 - live_row[...]
+        denominator = jnp.sum(exponent, axis=0, keepdims=True) + dead_row
         weight = (exponent / denominator).astype(BF16)
         probs[n] = weight
         o_cols[n] = dot(heads[2 * HEADS + n], weight)
@@ -492,7 +590,7 @@
             strips[t, pl.ds(p, SLOTS, stride=4), :] = merge_total[:, pl.ds(DV * p + 128 * t, 128)]
     for t in range(9):
         wide[:, pl.ds(128 * t, 128)] = strips[t]
-    og[1] = normalize_back(wide[...], h_out[...], r_out[...], merge_gain[...]).astype(BF16)
+    og[1] = normalize_back(wide[...], h_out[...], r_out[...], merge_gain).astype(BF16)
     halo_out = [
         copies.make(og.at[1], og.at[0], place.along(1)),
         copies.make(og.at[1], og.at[2], place.along(-1)),
@@ -506,6 +604,7 @@
                 proj[pl.ds(i * 384, 384), :], og[w], NT
             )
 
+    weights.finish((3,))
     project_back(1)
     for w, copy in ((0, halo_out[0]), (2, halo_out[1])):
         copy.wait_recv()
@@ -513,7 +612,7 @@
 
     own = pl.ds(PATCHES, PATCHES)
 
-    @pl.loop(0, HEADS)
+    @pl.loop(0, HEADS, unroll=2)
     def _(n):
         start = pl.multiple_of(n * HD, 8)
         upstream = t32[pl.ds(start, HD), :].astype(BF16)
@@ -533,9 +632,10 @@
         block = dot(qkv[pl.ds(i * 384, 384), :], projected_grad)
         wide[:, pl.ds(i * 384, 384)] = block.T
     out_ref[...] = (
-        og[1].astype(F32) + normalize_back(wide[...], h_in[...], r_in[...], ln_gain[...])
+        og[1].astype(F32) + normalize_back(wide[...], h_in[...], r_in[...], ln_gain)
     ).astype(BF16)
     copies.drain()
+    weights.drain()
 
 
 N_COPIES = 3 + 40 + 2 + 40 + 32 + 26 + 2
@@ -558,25 +658,6 @@
     fc1_bias,
     fc2_weight,
 ):
-    s = lax.axis_index("section")
-    v = lax.axis_index("vit")
-    section_weight = jnp.where(
-        section_layer < LEVELS, (section_layer + 1).astype(F32) / LEVELS, 0.0
-    ).reshape(1, 4)
-    counts = lax.dynamic_index_in_dim(image_rows, s, 0, keepdims=True)
-    order = jnp.arange(16, dtype=jnp.int32)
-    ends = jnp.sum(jnp.where(order[None, :] <= order[:, None], counts, 0), axis=1)
-    total = jnp.sum(counts)
-    slot_pos = lax.dynamic_slice_in_dim(vis_slot, s * 32, 32, 1).reshape(1, 512) - s * 512
-    live_slot = (jnp.arange(512, dtype=jnp.int32) < total).astype(F32)[:, None]
-    patch = v * PATCHES - PATCHES + jnp.arange(WINDOW, dtype=jnp.int32)
-    slot = patch >> 2
-    image = jnp.sum((slot[:, None] >= ends[None, :]).astype(jnp.int32), axis=1)
-    live = (patch >= 0) & (slot < total)
-    id_row = jnp.where(live, image, -1)[None, :]
-    id_col = jnp.where(live, image, -2)[:, None]
-    live_row = live.astype(F32)[None, :]
-
     anywhere = pl.BlockSpec(memory_space=pl.ANY)
     vmem = pl.BlockSpec(memory_space=pltpu.VMEM)
     smem = pl.BlockSpec(memory_space=pltpu.SMEM)
@@ -587,7 +668,7 @@
     return pl.pallas_call(
         body,
         out_shape=jax.ShapeDtypeStruct((PATCHES, DV), BF16),
-        in_specs=[anywhere] * 7 + [smem] + [vmem] * 10,
+        in_specs=[anywhere] * 13 + [smem] * 2,
         out_specs=vmem,
         scratch_shapes=[
             scratch((PATCHES, DV)),
@@ -623,9 +704,15 @@
             scratch((HEADS, HD, WINDOW), F32),
             scratch((3 * DV, PATCHES), F32),
             scratch((9, PATCHES, 128), F32),
+            scratch((DV,), F32),
+            scratch((DV,), F32),
+            scratch((DV,), F32),
+            scratch((DV,), F32),
+            scratch((HIDDEN,), F32),
+            scratch((16, 128), jnp.int32),
             pltpu.SemaphoreType.DMA((N_COPIES,)),
             pltpu.SemaphoreType.DMA((N_COPIES,)),
-            pltpu.SemaphoreType.DMA((7,)),
+            pltpu.SemaphoreType.DMA((13,)),
         ],
         compiler_params=pltpu.CompilerParams(
             collective_id=0, has_side_effects=True, vmem_limit_bytes=60 * 2**20
@@ -639,17 +726,14 @@
         proj_weight,
         fc1_weight.T,
         fc2_weight,
-        section_weight,
-        slot_pos,
-        live_slot,
-        id_row,
-        id_col,
-        live_row,
-        ln_gain.reshape(1, DV),
-        ln_bias.reshape(1, DV),
-        merge_gain.reshape(1, DV),
-        merge_bias.reshape(1, DV),
-        fc1_bias.reshape(1, HIDDEN),
+        ln_gain,
+        ln_bias,
+        merge_gain,
+        merge_bias,
+        fc1_bias,
+        vis_slot,
+        image_rows,
+        section_layer,
     )
 
 

time: 233 us -> 153 us (0.66); the launches traced: 229 us -> 153 us
  Pallas kernels: 211 us -> 152 us
  other arithmetic: 9.04 us -> 0 us
  local copies, waits for them, and re-layouts: 8.78 us -> 1.7 us
    pallas_call x1, Pallas kernels: 211 us -> 152 us  [local(): pl.pallas_call(body, out_shape=jax.ShapeDtypeStruct((PATCHES, DV), BF16),...]
    reshape x5 -> x0, local copies, waits for them, and re-layouts: 6.42 us -> none  [the longest x1 1.29 us: local(): ln_gain.reshape(1, DV)]
    select_n x2 -> x0, other arithmetic: 2.71 us -> none  [the longest x1 1.48 us: local(): id_col = jnp.where(live, image, -2)[:, None]]
    convert_element_type x2 -> x0, other arithmetic: 2.71 us -> none  [the longest x1 1.42 us: local(): live_slot = (jnp.arange(512, dtype=jnp.int32) < total).astype(F32)[:, None]]
where the time goes in v2:
time: 153 us
  Pallas kernels  152 us (99%)
  local copies, waits for them, and re-layouts  1.7 us (1%)
    pallas_call x1, Pallas kernels, local(): pl.pallas_call(body, out_shape=jax.ShapeDtypeStruct((PATCHES, DV), BF16),...  152 us

profile of v2, /device:TPU:64, one launch (start us, length us, event | category | flops | bytes accessed | tf_op | source)
XLA Modules:
  0.0 153.2 jit_solution(3332596284387855247)
XLA Ops:
  0.0 151.5 %merger_and_attention.1 = bf16[128,1152]{1,0:T(8,128)(2,1)} custom-call(bf16[128,4096]{1,0:T(8,128)(2,1)} %bitcast.3, bf16[128,1152]{1,0:T(8,128)(2,1)} %vit_in.1, bf16[128,1152]{1,0:T(8,128)(2,1)} %vit_out.1, bf16[288,3456]{1,0:T(8,128)(2,1)} %qkv_w.1, bf16[288,1152]{1,0:T(8,128)(2,1)} %proj_w.1, bf16[288,4608]{1,0:T(8,128)(2,1)} %bitcast.2, ...), custom_call_target="tpu_custom_call" | custom-call | tf_op jit(solution)/shard_map/merger_and_attention/pallas_call | solution.py:668
  151.5 1.7 %copy.17 = bf16[128,1152]{1,0:T(8,128)(2,1)} copy(bf16[128,1152]{1,0:T(8,128)(2,1)} %merger_and_attention.1) | data formatting | bytes 589824

commit v3 on v2

--- a/solution.py
+++ b/solution.py
@@ -306,7 +306,7 @@
         for k, (src, dst) in enumerate((
             (vit_out, xo),
             (grad.at[group_rows], zown),
-            (vit_in, xin.at[1]),
+            (vit_in, xin.at[0]),
             (fc1_w, fc1),
             (qkv_w, qkv.at[own_rows]),
             (proj_w, proj.at[own_rows]),
@@ -349,7 +349,7 @@
     gather_in = PlaneGather(place, copies, rows_in, DM, HALF)
     gather_in.start()
     halo_in = [
-        copies.make(vit_in, xin.at[0], place.along(1)),
+        copies.make(vit_in, xin.at[1], place.along(1)),
         copies.make(vit_in, xin.at[2], place.along(-1)),
     ]
     gather_grad = PlaneGather(place, copies, rows_grad, DL, DL // 2)
@@ -405,23 +405,25 @@
     gather_grad.pass_on(0)
     gather_grad.far()
     fill_slope(2, 4)
-    weights.step(3)
     gather_grad.pass_on(-1)
     gather_grad.pass_on(1)
-    weights.step(4)
     gather_grad.pass_on(2)
+    weights.step(3)
     for k in (2, 6, 9, 10, 12):
         local[k].wait()
+
+    def fill_hidden(offsets):
+        blocks = [lax.rem(y + dy + 4, 4) * 4 + lax.rem(x + dx + 4, 4) for dx, dy in offsets]
+        rows = jnp.concatenate([rows_grad[i] for i in blocks], axis=0)
+        product = dot(rows, fc2[...], NT)
+        for k, i in enumerate(blocks):
+            hidden[pl.ds(pl.multiple_of(i * 32, 32), 32), :] = product[32 * k : 32 * k + 32]
+
+    for dy in (0, -1, 1):
+        fill_hidden([(dx, dy) for dx in (0, -1, 1)])
     gather_grad.finish()
-
-    @pl.loop(0, 4)
-    def _(i):
-        block = rows_grad[pl.ds(i * 4, 4)].reshape(128, DL)
-        rows = pl.ds(pl.multiple_of(i * 128, 128), 128)
-        hidden[rows, :] = dot(block, fc2[...], NT)
-
-
-    weights.step(5)
+    fill_hidden([(dx, 2) for dx in (0, -1, 1, 2)])
+    fill_hidden([(2, dy) for dy in (0, -1, 1)])
 
     ends = []
     for k in range(16):
@@ -495,6 +497,7 @@
         for k in (0, 1):
             sums[part]["2m"][k].start()
 
+    weights.step(4)
     def add(part, d1, k, got):
         ps[part, d1, k] = (ps[part, d1, k].astype(F32) + got[...].astype(F32)).astype(BF16)
 
@@ -509,8 +512,8 @@
             sums[part]["2m"][k].start()
     for part in (0, 1):
         product(part, 0)
-
-    weights.step(6)
+    weights.step(5)
+
     for copy in halo_in:
         copy.wait_recv()
     ln_gain = ln_gain_v[...].reshape(1, DV)
@@ -518,7 +521,7 @@
 
     for w in range(3):
         h, r = normalize(xin[w].astype(F32))
-        if w == 1:
+        if w == 0:
             h_in[...] = h
             r_in[...] = r
         xin[w] = (h * ln_gain + ln_bias).astype(BF16)
@@ -558,7 +561,9 @@
 
     def image_of(axis):
         shape = (1, WINDOW) if axis else (WINDOW, 1)
-        patch = lax.broadcasted_iota(jnp.int32, shape, axis) + (place.v * PATCHES - PATCHES)
+        index = lax.broadcasted_iota(jnp.int32, shape, axis)
+        back = jnp.where(index < PATCHES, 0, jnp.where(index < 2 * PATCHES, 2 * PATCHES, PATCHES))
+        patch = index - back + place.v * PATCHES
         slot = patch >> 2
         image = jnp.zeros(shape, jnp.int32)
         for end in ends:
@@ -590,10 +595,10 @@
             strips[t, pl.ds(p, SLOTS, stride=4), :] = merge_total[:, pl.ds(DV * p + 128 * t, 128)]
     for t in range(9):
         wide[:, pl.ds(128 * t, 128)] = strips[t]
-    og[1] = normalize_back(wide[...], h_out[...], r_out[...], merge_gain).astype(BF16)
+    og[0] = normalize_back(wide[...], h_out[...], r_out[...], merge_gain).astype(BF16)
     halo_out = [
-        copies.make(og.at[1], og.at[0], place.along(1)),
-        copies.make(og.at[1], og.at[2], place.along(-1)),
+        copies.make(og.at[0], og.at[1], place.along(1)),
+        copies.make(og.at[0], og.at[2], place.along(-1)),
     ]
     for copy in halo_out:
         copy.start()
@@ -604,35 +609,49 @@
                 proj[pl.ds(i * 384, 384), :], og[w], NT
             )
 
+    weights.step(6)
     weights.finish((3,))
-    project_back(1)
-    for w, copy in ((0, halo_out[0]), (2, halo_out[1])):
+    project_back(0)
+
+    own, others = pl.ds(0, PATCHES), pl.ds(PATCHES, 2 * PATCHES)
+
+    def places(n):
+        start = pl.multiple_of(n * HD, 8)
+        return [pl.ds(pl.multiple_of(start + j * DV, 8), HD) for j in range(3)]
+
+    @pl.loop(0, HEADS, unroll=4)
+    def _(n):
+        query, key, value = places(n)
+        upstream = t32[query, own].astype(BF16)
+        delta = jnp.sum(upstream.astype(F32) * o_cols[n, :, own], axis=0, keepdims=True)
+        weight = probs[n, :, own]
+        prob = dot(v_rows[n], upstream)
+        score = (weight.astype(F32) * (prob - delta) * SCALE).astype(BF16)
+        pg[query, :] = dot(heads[HEADS + n], score)
+        pg[key, :] = dot(heads[n, :, own], score[:PATCHES], NT)
+        pg[value, :] = dot(upstream, weight[:PATCHES], NT)
+
+    for w, copy in ((1, halo_out[0]), (2, halo_out[1])):
         copy.wait_recv()
         project_back(w)
 
-    own = pl.ds(PATCHES, PATCHES)
-
-    @pl.loop(0, HEADS, unroll=2)
+    @pl.loop(0, HEADS, unroll=4)
     def _(n):
-        start = pl.multiple_of(n * HD, 8)
-        upstream = t32[pl.ds(start, HD), :].astype(BF16)
-        delta = jnp.sum(upstream.astype(F32) * o_cols[n], axis=0, keepdims=True)
-        prob1 = dot(v_rows[n], upstream[:, PATCHES : 2 * PATCHES])
-        weight1 = probs[n, :, own].astype(F32)
-        score1 = weight1 * (prob1 - delta[:, PATCHES : 2 * PATCHES]) * SCALE
-        pg[pl.ds(start, HD), :] = dot(heads[HEADS + n], score1.astype(BF16))
-        prob2 = dot(v_rows[n, own, :], upstream)
-        weight2 = probs[n, own, :]
-        score2 = (weight2.astype(F32) * (prob2 - delta) * SCALE).astype(BF16)
-        pg[pl.ds(pl.multiple_of(start + DV, 8), HD), :] = dot(heads[n], score2, NT)
-        pg[pl.ds(pl.multiple_of(start + 2 * DV, 8), HD), :] = dot(upstream, weight2, NT)
+        query, key, value = places(n)
+        upstream = t32[query, others].astype(BF16)
+        delta = jnp.sum(upstream.astype(F32) * o_cols[n, :, others], axis=0, keepdims=True)
+        weight = probs[n, own, others]
+        prob = dot(v_rows[n, own, :], upstream)
+        score = (weight.astype(F32) * (prob - delta) * SCALE).astype(BF16)
+        pg[key, :] += dot(heads[n, :, others], score, NT)
+        pg[value, :] += dot(upstream, weight, NT)
 
     projected_grad = pg[...].astype(BF16)
     for i in range(3):
         block = dot(qkv[pl.ds(i * 384, 384), :], projected_grad)
         wide[:, pl.ds(i * 384, 384)] = block.T
     out_ref[...] = (
-        og[1].astype(F32) + normalize_back(wide[...], h_in[...], r_in[...], ln_gain)
+        og[0].astype(F32) + normalize_back(wide[...], h_in[...], r_in[...], ln_gain)
     ).astype(BF16)
     copies.drain()
     weights.drain()

time: 153 us -> 136 us (0.89); the launches traced: 153 us -> 134 us
  Pallas kernels: 152 us -> 133 us
    pallas_call x1, Pallas kernels: 152 us -> 133 us  [local(): pl.pallas_call(body, out_shape=jax.ShapeDtypeStruct((PATCHES, DV), BF16),...]
where the time goes in v3:
time: 136 us; the launch traced here: 134 us
  Pallas kernels  133 us (98%)
  local copies, waits for them, and re-layouts  1.7 us (1%)
    pallas_call x1, Pallas kernels, local(): pl.pallas_call(body, out_shape=jax.ShapeDtypeStruct((PATCHES, DV), BF16),...  133 us

profile of v3, /device:TPU:64, one launch (start us, length us, event | category | flops | bytes accessed | tf_op | source)
XLA Modules:
  0.0 134.5 jit_solution(16285148319464592404)
XLA Ops:
  0.0 132.8 %merger_and_attention.1 = bf16[128,1152]{1,0:T(8,128)(2,1)} custom-call(bf16[128,4096]{1,0:T(8,128)(2,1)} %bitcast.3, bf16[128,1152]{1,0:T(8,128)(2,1)} %vit_in.1, bf16[128,1152]{1,0:T(8,128)(2,1)} %vit_out.1, bf16[288,3456]{1,0:T(8,128)(2,1)} %qkv_w.1, bf16[288,1152]{1,0:T(8,128)(2,1)} %proj_w.1, bf16[288,4608]{1,0:T(8,128)(2,1)} %bitcast.2, ...), custom_call_target="tpu_custom_call" | custom-call | tf_op jit(solution)/shard_map/merger_and_attention/pallas_call | solution.py:687
  132.8 1.7 %copy.17 = bf16[128,1152]{1,0:T(8,128)(2,1)} copy(bf16[128,1152]{1,0:T(8,128)(2,1)} %merger_and_attention.1) | data formatting | bytes 589824

commit v4 on v3

--- a/solution.py
+++ b/solution.py
@@ -407,9 +407,23 @@
     fill_slope(2, 4)
     gather_grad.pass_on(-1)
     gather_grad.pass_on(1)
+    for k in (2, 9, 10):
+        local[k].wait()
+    for copy in halo_in:
+        copy.wait_recv()
+    ln_gain = ln_gain_v[...].reshape(1, DV)
+    ln_bias = ln_bias_v[...].reshape(1, DV)
+
+    for w in range(3):
+        h, r = normalize(xin[w].astype(F32))
+        if w == 0:
+            h_in[...] = h
+            r_in[...] = r
+        xin[w] = (h * ln_gain + ln_bias).astype(BF16)
+
     gather_grad.pass_on(2)
     weights.step(3)
-    for k in (2, 6, 9, 10, 12):
+    for k in (6, 12):
         local[k].wait()
 
     def fill_hidden(offsets):
@@ -514,24 +528,12 @@
         product(part, 0)
     weights.step(5)
 
-    for copy in halo_in:
-        copy.wait_recv()
-    ln_gain = ln_gain_v[...].reshape(1, DV)
-    ln_bias = ln_bias_v[...].reshape(1, DV)
-
-    for w in range(3):
-        h, r = normalize(xin[w].astype(F32))
-        if w == 0:
-            h_in[...] = h
-            r_in[...] = r
-        xin[w] = (h * ln_gain + ln_bias).astype(BF16)
-
     def attend(j):
         for i in range(3):
             block = dot(xin[...].reshape(WINDOW, DV), qkv[:, pl.ds(j * DV + i * 384, 384)])
             t32[pl.ds(i * 384, 384), :] = block.T
 
-        @pl.loop(0, HEADS, unroll=2)
+        @pl.loop(0, HEADS, unroll=4)
         def _(n):
             cols = t32[pl.ds(pl.multiple_of(n * HD, 8), HD), :]
             heads[j * HEADS + n] = cols.astype(BF16)
@@ -542,6 +544,8 @@
 
     weights.finish((0, 1, 2))
     attend(0)
+    attend(1)
+    attend(2)
     for k in (2, 3, 1, 0):
         for part in (0, 1):
             sums[part]["2p"][k].wait_recv()
@@ -556,8 +560,6 @@
                 sums[part]["3"][k - 1].start()
             else:
                 merge_total[:, pl.ds(part * HALF, HALF)] = total
-    attend(1)
-    attend(2)
 
     def image_of(axis):
         shape = (1, WINDOW) if axis else (WINDOW, 1)
@@ -575,7 +577,7 @@
     id_col, _ = image_of(0)
     dead_row = jnp.where(live_row, 0.0, 1.0)
 
-    @pl.loop(0, HEADS, unroll=2)
+    @pl.loop(0, HEADS, unroll=4)
     def _(n):
         scores = dot(k_rows[n], heads[n]) * SCALE
         allowed = id_col == id_row

time: 136 us -> 133 us (0.978)
  Pallas kernels: 133 us -> 130 us
    pallas_call x1, Pallas kernels: 133 us -> 130 us  [local(): pl.pallas_call(body, out_shape=jax.ShapeDtypeStruct((PATCHES, DV), BF16),...]
where the time goes in v4:
time: 133 us; the launch traced here: 131 us
  Pallas kernels  130 us (98%)
  local copies, waits for them, and re-layouts  1.7 us (1%)
    pallas_call x1, Pallas kernels, local(): pl.pallas_call(body, out_shape=jax.ShapeDtypeStruct((PATCHES, DV), BF16),...  130 us

profile of v4, /device:TPU:64, one launch (start us, length us, event | category | flops | bytes accessed | tf_op | source)
XLA Modules:
  0.0 131.4 jit_solution(18416927290832374405)
XLA Ops:
  0.0 129.6 %merger_and_attention.1 = bf16[128,1152]{1,0:T(8,128)(2,1)} custom-call(bf16[128,4096]{1,0:T(8,128)(2,1)} %bitcast.3, bf16[128,1152]{1,0:T(8,128)(2,1)} %vit_in.1, bf16[128,1152]{1,0:T(8,128)(2,1)} %vit_out.1, bf16[288,3456]{1,0:T(8,128)(2,1)} %qkv_w.1, bf16[288,1152]{1,0:T(8,128)(2,1)} %proj_w.1, bf16[288,4608]{1,0:T(8,128)(2,1)} %bitcast.2, ...), custom_call_target="tpu_custom_call" | custom-call | tf_op jit(solution)/shard_map/merger_and_attention/pallas_call | solution.py:689
  129.7 1.7 %copy.17 = bf16[128,1152]{1,0:T(8,128)(2,1)} copy(bf16[128,1152]{1,0:T(8,128)(2,1)} %merger_and_attention.1) | data formatting | bytes 589824

commit v5 on v4

--- a/solution.py
+++ b/solution.py
@@ -633,6 +633,11 @@
         pg[key, :] = dot(heads[n, :, own], score[:PATCHES], NT)
         pg[value, :] = dot(upstream, weight[:PATCHES], NT)
 
+    query_grad = pg[pl.ds(0, DV), :].astype(BF16)
+    for i in range(3):
+        rows = pl.ds(i * 384, 384)
+        t32[rows, own] = dot(qkv[rows, pl.ds(0, DV)], query_grad)
+
     for w, copy in ((1, halo_out[0]), (2, halo_out[1])):
         copy.wait_recv()
         project_back(w)
@@ -648,10 +653,11 @@
         pg[key, :] += dot(heads[n, :, others], score, NT)
         pg[value, :] += dot(upstream, weight, NT)
 
-    projected_grad = pg[...].astype(BF16)
+    key_value_grad = pg[pl.ds(DV, 2 * DV), :].astype(BF16)
     for i in range(3):
-        block = dot(qkv[pl.ds(i * 384, 384), :], projected_grad)
-        wide[:, pl.ds(i * 384, 384)] = block.T
+        rows = pl.ds(i * 384, 384)
+        block = t32[rows, own] + dot(qkv[rows, pl.ds(DV, 2 * DV)], key_value_grad)
+        wide[:, rows] = block.T
     out_ref[...] = (
         og[0].astype(F32) + normalize_back(wide[...], h_in[...], r_in[...], ln_gain)
     ).astype(BF16)

time: 133 us -> 133 us (level)
  no operation moved by 1% of the time
where the time goes in v5:
time: 133 us; the launch traced here: 131 us
  Pallas kernels  129 us (97%)
  local copies, waits for them, and re-layouts  1.7 us (1%)
    pallas_call x1, Pallas kernels, local(): pl.pallas_call(body, out_shape=jax.ShapeDtypeStruct((PATCHES, DV), BF16),...  129 us

profile of v5, /device:TPU:64, one launch (start us, length us, event | category | flops | bytes accessed | tf_op | source)
XLA Modules:
  0.0 130.7 jit_solution(3282520019527867292)
XLA Ops:
  0.0 129.0 %merger_and_attention.1 = bf16[128,1152]{1,0:T(8,128)(2,1)} custom-call(bf16[128,4096]{1,0:T(8,128)(2,1)} %bitcast.3, bf16[128,1152]{1,0:T(8,128)(2,1)} %vit_in.1, bf16[128,1152]{1,0:T(8,128)(2,1)} %vit_out.1, bf16[288,3456]{1,0:T(8,128)(2,1)} %qkv_w.1, bf16[288,1152]{1,0:T(8,128)(2,1)} %proj_w.1, bf16[288,4608]{1,0:T(8,128)(2,1)} %bitcast.2, ...), custom_call_target="tpu_custom_call" | custom-call | tf_op jit(solution)/shard_map/merger_and_attention/pallas_call | solution.py:695
  129.0 1.7 %copy.17 = bf16[128,1152]{1,0:T(8,128)(2,1)} copy(bf16[128,1152]{1,0:T(8,128)(2,1)} %merger_and_attention.1) | data formatting | bytes 589824
